TPU v7x, 256 devices: a whole 4x4x8 slice. The times are simulated.
256 devices in a mesh: gx: 8 (over y, z_hi), gy: 8 (over x, core), gz: 4 (over z_lo).
Axes of the slice: x: 4, y: 4, z: 8 (z_hi: 2, z_lo: 4; z = z_hi * 4 + z_lo), core: 2. Of those that a mesh axis runs over, the one named last changes fastest.
Arguments:
- tokens: bfloat16 [1024, 4096], P(('gy', 'gx'), 'gz'), may hold values from -6 to 6
- gate_weight: bfloat16 [4096, 14784], P(('gz', 'gy'), 'gx'), may hold values from -0.09375 to 0.09375
- up_weight: bfloat16 [4096, 14784], P(('gz', 'gy'), 'gx'), may hold values from -0.09375 to 0.09375
- down_weight: bfloat16 [14784, 4096], P(('gx', 'gy'), 'gz'), may hold values from -0.046875 to 0.046875
- cotangent: bfloat16 [1024, 4096], P(('gy', 'gx'), 'gz'), may hold values from -6 to 6
Outputs:
- mixed: bfloat16 [1024, 4096], P(('gy', 'gx'), 'gz')
- grad_tokens: bfloat16 [1024, 4096], P(('gy', 'gx'), 'gz')
- grad_gate: float32 [4096, 14784], P(('gz', 'gy'), 'gx')
- grad_up: float32 [4096, 14784], P(('gz', 'gy'), 'gx')
- grad_down: float32 [14784, 4096], P(('gx', 'gy'), 'gz')
All inputs are finite; a program needn't handle non-finite values.
Results may differ from a plain program's by a relative error of at most 0.005.
Values may be sent and summed in bfloat16 or wider, within the bound.
A program may use at most 128 MiB of HBM per device.

v0:
```python
import math

import jax
import jax.numpy as jnp
from jax import lax
from jax.sharding import PartitionSpec as P


def contract_last(left, right):
    return lax.dot_general(
        left, right, (((1,), (1,)), ((), ())), preferred_element_type=jnp.float32
    )


def contract_first(left, right):
    return lax.dot_general(
        left, right, (((0,), (0,)), ((), ())), preferred_element_type=jnp.float32
    )


def body(tokens, gate_weight, up_weight, down_weight, cotangent):
    width_hidden = gate_weight.shape[1]
    token_block = lax.all_gather(tokens, "gx", axis=0, tiled=True)
    rows_group = token_block.shape[0]
    paired = jnp.concatenate([gate_weight, up_weight], axis=1)
    paired_full = lax.all_gather(paired, "gy", axis=0, tiled=True)
    piece = token_block
    gate_up = lax.psum_scatter(
        jnp.dot(piece, paired_full, preferred_element_type=jnp.float32),
        "gz",
        scatter_dimension=0,
        tiled=True,
    )
    gate = gate_up[:, :width_hidden]
    up = gate_up[:, width_hidden:]
    sigma = jax.nn.sigmoid(gate)
    swish = gate * sigma
    hidden = (swish * up).astype(jnp.bfloat16)
    hidden_block = lax.all_gather(hidden, "gz", axis=0, tiled=True)
    grad_block = lax.all_gather(cotangent, "gx", axis=0, tiled=True)
    down_full = lax.all_gather(down_weight, "gy", axis=0, tiled=True)
    piece = hidden_block
    mixed = lax.psum_scatter(
        jnp.dot(piece, down_full, preferred_element_type=jnp.float32),
        "gx",
        scatter_dimension=0,
        tiled=True,
    )
    piece = grad_block
    grad_hidden = lax.psum_scatter(
        contract_last(piece, down_full), "gz", scatter_dimension=0, tiled=True
    )
    mixed = mixed.astype(jnp.bfloat16)
    slope = sigma * (1.0 + gate * (1.0 - sigma))
    grad_gate_act = (grad_hidden * up * slope).astype(jnp.bfloat16)
    grad_up_act = (grad_hidden * swish).astype(jnp.bfloat16)
    grad_pair = jnp.concatenate([grad_gate_act, grad_up_act], axis=1)
    grad_pair_block = lax.all_gather(grad_pair, "gz", axis=0, tiled=True)
    piece = grad_pair_block
    grad_tokens = lax.psum_scatter(
        contract_last(piece, paired_full), "gx", scatter_dimension=0, tiled=True
    ).astype(jnp.bfloat16)
    factor = 1.0 / math.sqrt(rows_group * lax.axis_size("gy"))
    columns = token_block
    grad_pair_weight = lax.psum_scatter(
        contract_first(columns, grad_pair_block) * factor, "gy", scatter_dimension=0, tiled=True
    )
    grad_gate = grad_pair_weight[:, :width_hidden]
    grad_up = grad_pair_weight[:, width_hidden:]
    columns = hidden_block
    grad_down = lax.psum_scatter(
        contract_first(columns, grad_block) * factor, "gy", scatter_dimension=0, tiled=True
    )
    return (mixed, grad_tokens, grad_gate, grad_up, grad_down)


def solution(mesh):
    in_specs = (
        P(("gy", "gx"), "gz"),
        P(("gz", "gy"), "gx"),
        P(("gz", "gy"), "gx"),
        P(("gx", "gy"), "gz"),
        P(("gy", "gx"), "gz"),
    )
    out_specs = (
        P(("gy", "gx"), "gz"),
        P(("gy", "gx"), "gz"),
        P(("gz", "gy"), "gx"),
        P(("gz", "gy"), "gx"),
        P(("gx", "gy"), "gz"),
    )
    return jax.shard_map(body, mesh=mesh, in_specs=in_specs, out_specs=out_specs, check_vma=False)
```

profile of v0, /device:TPU:40, one launch (start us, length us, event | category | flops | bytes accessed | tf_op | source)
XLA Modules:
  0.0 468.2 jit_solution(3914233677406422871)
XLA Ops:
  7.2 0.0 all-gather.6.cloned.1.call-start
  7.2 0.7 all-gather.6.cloned.1.call-update
  7.9 0.0 all-gather.4.cloned.1.call-start
  7.9 2.2 pad_maximum_fusion
  10.1 0.0 copy-start
  10.1 0.0 all-gather.4.cloned.1.call-update
  10.1 0.0 reduce-scatter.20.cloned.1.call-start
  10.2 44.0 %all_gather.22 = bf16[128,1024]{1,0:T(8,128)(2,1)S(1)} all-gather(bf16[16,1024]{1,0:T(8,128)(2,1)} %param.9), channel_id=1, replica_groups=mesh['gx'=8,'gy'=8,'gz'=4] {'gx'}, dimensions={0}, use_global_device_ids=true | all-gather | bytes 294912 | tf_op jit(solution)/shard_map/all_gather | solution.py:40
  54.1 0.0 all-gather.6.cloned.1.call-done
  54.1 5.1 %reshape.11 = bf16[1848,1024]{1,0:T(8,128)(2,1)} reshape(bf16[8,231,1024]{2,1,0:T(8,128)(2,1)} %all-gather.6.cloned.1.call-done) | data formatting | bytes 7569408
  59.3 4.8 %fusion.4 = f32[128,1848]{1,0:T(8,128)} fusion(bf16[128,1024]{1,0:T(8,128)(2,1)S(1)} %all_gather.22, bf16[1848,1024]{1,0:T(8,128)(2,1)} %reshape.11), kind=kOutput, calls=%fused_computation.13 | convolution fusion | flops 484442112 | bytes 4993024
  64.0 0.0 reduce-scatter.20.cloned.1.call-update
  64.0 0.0 reduce-scatter.18.cloned.1.call-start
  64.1 0.0 copy-done
  64.1 45.1 %all_gather.19 = bf16[128,1024]{1,0:T(8,128)(2,1)S(1)} all-gather(bf16[16,1024]{1,0:T(8,128)(2,1)S(1)} %copy-done), channel_id=1, replica_groups=mesh['gx'=8,'gy'=8,'gz'=4] {'gx'}, dimensions={0}, use_global_device_ids=true | all-gather | bytes 294912 | tf_op jit(solution)/shard_map/all_gather | solution.py:23
  109.2 0.0 all-gather.4.cloned.1.call-done
  109.2 5.3 %convolution_bitcast_fusion = f32[128,3696]{0,1:T(8,128)S(1)} fusion(bf16[1024,3696]{0,1:T(8,128)(2,1)} %all-gather.4.cloned.1.call-done, bf16[128,1024]{1,0:T(8,128)(2,1)S(1)} %all_gather.19), kind=kOutput, calls=%fused_computation.1 | convolution fusion | flops 968884224 | bytes 9723904 | tf_op jit(solution)/shard_map/dot_general | solution.py:29
  114.5 2.2 copy.22
  116.8 0.0 reduce-scatter.18.cloned.1.call-update
  116.8 0.0 reduce-scatter.12.cloned.1.call-start
  116.8 16.7 %reduce-scatter.20.cloned.1.call-done = f32[32,1848]{1,0:T(8,128)} async-done(((f32[128,1848]{1,0:T(8,128)}), f32[32,1848]{1,0:T(8,128)}) %reduce-scatter.20.cloned.1.call-update) | async-done | bytes 236560 | tf_op jit(solution)/shard_map/reduce_scatter | solution.py:50
  133.5 48.6 %reduce-scatter.18.cloned.1.call-done = f32[32,3696]{1,0:T(8,128)} async-done(((f32[128,3696]{1,0:T(8,128)}), f32[32,3696]{1,0:T(8,128)}) %reduce-scatter.18.cloned.1.call-update) | async-done | bytes 473104 | tf_op jit(solution)/shard_map/reduce_scatter | solution.py:28
  182.2 1.3 multiply_convert_fusion.1
  183.5 13.9 %all_gather.20 = bf16[128,1848]{1,0:T(8,128)(2,1)S(1)} all-gather(bf16[32,1848]{1,0:T(8,128)(2,1)S(1)} %get-tuple-element.9), channel_id=1, replica_groups=mesh['gx'=8,'gy'=8,'gz'=4] {'gz'}, dimensions={0}, use_global_device_ids=true | all-gather | bytes 591360 | tf_op jit(solution)/shard_map/all_gather | solution.py:39
  197.4 3.7 fusion.3
  201.1 0.0 reduce-scatter.12.cloned.1.call-update
  201.1 0.0 reduce-scatter.14.cloned.1.call-start
  201.1 0.1 pad_maximum_fusion.1
  201.2 20.1 %all_gather.23 = bf16[128,3696]{1,0:T(8,128)(2,1)S(1)} all-gather(bf16[32,3696]{1,0:T(8,128)(2,1)S(1)} %pad_maximum_fusion.1), channel_id=1, replica_groups=mesh['gx'=8,'gy'=8,'gz'=4] {'gz'}, dimensions={0}, use_global_device_ids=true | all-gather | bytes 1182720 | tf_op jit(solution)/shard_map/all_gather | solution.py:58
  221.4 5.2 %fusion.5 = f32[128,1024]{1,0:T(8,128)} fusion(bf16[128,3696]{1,0:T(8,128)(2,1)S(1)} %all_gather.23, bf16[1024,3696]{0,1:T(8,128)(2,1)} %all-gather.4.cloned.1.call-done), kind=kOutput, calls=%fused_computation.14 | convolution fusion | flops 968884224 | bytes 9039872 | tf_op jit(solution)/shard_map/dot_general | solution.py:10
  226.5 0.0 reduce-scatter.14.cloned.1.call-update
  226.6 0.0 reduce-scatter.16.cloned.1.call-start
  226.6 7.5 %multiply_bitcast_fusion = f32[1024,3696]{0,1:T(8,128)} fusion(bf16[128,3696]{1,0:T(8,128)(2,1)S(1)} %all_gather.23, bf16[128,1024]{1,0:T(8,128)(2,1)S(1)} %all_gather.19), kind=kOutput, calls=%fused_computation | convolution fusion | flops 972668928 | bytes 16347136 | tf_op jit(solution)/shard_map/dot_general | solution.py:16
  234.1 0.0 reduce-scatter.16.cloned.1.call-update
  234.1 0.0 copy-start.1
  234.1 4.2 convolution_multiply_fusion
  238.3 47.9 %fusion = f32[232,1024]{1,0:T(8,128)S(1)} fusion(f32[1848,1024]{1,0:T(8,128)} %convolution_multiply_fusion), kind=kCustom, calls=%all-reduce-scatter | all-reduce-scatter fusion | flops 1900545 | bytes 8520704
  286.3 1.3 collective-permute-start
  287.6 0.0 copy-done.1
  287.6 0.6 dynamic-slice.4
  288.8 0.0 collective-permute-done
  288.8 0.7 concatenate.8
  289.5 1.1 constant_dynamic-slice_fusion
  290.6 0.0 reduce-scatter.12.cloned.1.call-done
  290.6 1.5 convert_element_type.16
  292.0 79.5 %reduce-scatter.14.cloned.1.call-done = f32[16,1024]{1,0:T(8,128)} async-done(((f32[128,1024]{1,0:T(8,128)}), f32[16,1024]{1,0:T(8,128)}) %reduce-scatter.14.cloned.1.call-update) | async-done | bytes 65552 | tf_op jit(solution)/shard_map/reduce_scatter | solution.py:60
  371.5 1.5 convert_element_type.19
  373.0 85.5 %reduce-scatter.16.cloned.1.call-done = f32[128,3696]{0,1:T(8,128)} async-done(((f32[1024,3696]{0,1:T(8,128)}), f32[128,3696]{0,1:T(8,128)}) %reduce-scatter.16.cloned.1.call-update) | async-done | bytes 1892368 | tf_op jit(solution)/shard_map/reduce_scatter | solution.py:65
  458.5 2.8 fusion.2
  (1 shorter events, 0.0 us)
Async XLA Ops:
  7.2 47.0 %all-gather.6.cloned.1.call-start = ((), (), s32[]{:S(2)}) async-start(), calls=%async_computation.9 | async-start | bytes 4276224 | tf_op jit(solution)/shard_map/all_gather | solution.py:41
  7.9 101.3 %all-gather.4.cloned.1.call-start = ((), (), s32[]{:S(2)}) async-start(), calls=%async_computation.5 | async-start | bytes 8515584 | tf_op jit(solution)/shard_map/all_gather | solution.py:26
  10.1 54.0 %copy-start = (bf16[16,1024]{1,0:T(8,128)(2,1)S(1)}, bf16[16,1024]{1,0:T(8,128)(2,1)}, u32[]{:S(2)}) copy-start(bf16[16,1024]{1,0:T(8,128)(2,1)} %param.5) | copy-start | bytes 98308
  10.1 123.4 %reduce-scatter.20.cloned.1.call-start = ((), (), s32[]{:S(2)}) async-start(), calls=%async_computation.11 | async-start | bytes 1228800 | tf_op jit(solution)/shard_map/reduce_scatter | solution.py:50
  64.0 118.2 %reduce-scatter.18.cloned.1.call-start = ((), (), s32[]{:S(2)}) async-start(), calls=%async_computation.10 | async-start | bytes 2375680 | tf_op jit(solution)/shard_map/reduce_scatter | solution.py:28
  116.8 173.8 %reduce-scatter.12.cloned.1.call-start = ((), (), s32[]{:S(2)}) async-start(), calls=%async_computation.6 | async-start | bytes 589824 | tf_op jit(solution)/shard_map/reduce_scatter | solution.py:43
  201.1 170.5 %reduce-scatter.14.cloned.1.call-start = ((), (), s32[]{:S(2)}) async-start(), calls=%async_computation.7 | async-start | bytes 589824 | tf_op jit(solution)/shard_map/reduce_scatter | solution.py:60
  226.6 232.0 %reduce-scatter.16.cloned.1.call-start = ((), (), s32[]{:S(2)}) async-start(), calls=%async_computation.8 | async-start | bytes 17031168 | tf_op jit(solution)/shard_map/reduce_scatter | solution.py:65
  234.1 53.5 %copy-start.1 = (u32[256]{0:T(256)S(1)}, u32[256]{0:T(256)}, u32[]{:S(2)}) copy-start(u32[256]{0:T(256)} %constant.10) | copy-start | bytes 3076
  286.3 2.5 collective-permute-start
Sparse Core Ops, SparseCore 0:
  9.8 35.5 all-gather.5
  47.8 52.8 all-gather.3
  103.3 30.2 reduce-scatter.19
  136.1 46.0 reduce-scatter.17
  201.2 85.0 reduce-scatter.11
  291.1 80.3 reduce-scatter.13
  374.1 84.3 reduce-scatter.15
where the time goes:
time: 470 us; the launch traced here: 468 us
  waiting for transfers between devices  231 us (49%)
  blocking collectives  171 us (36%)
  matrix products  30.5 us (6%)
  between operations  14.9 us (3%)
  local copies, waits for them, and re-layouts  12.5 us (3%)
  other arithmetic  6.51 us (1%)
    reduce_scatter x1, waiting for transfers between devices, body(): lax.psum_scatter(contract_first(columns, grad_pair_block) * factor, 'gy',...  85.5 us
    reduce_scatter x1, waiting for transfers between devices, body(): lax.psum_scatter(contract_last(piece, paired_full), 'gx', scatter_dimensi...  79.5 us
    reduce_scatter x1, waiting for transfers between devices, body(): lax.psum_scatter(jnp.dot(piece, paired_full, preferred_element_type=jnp.f...  48.6 us
    unnamed x1, blocking collectives  47.9 us
    all_gather x1, blocking collectives, body(): token_block = lax.all_gather(tokens, 'gx', axis=0, tiled=True)  45.1 us
    all_gather x1, blocking collectives, body(): grad_block = lax.all_gather(cotangent, 'gx', axis=0, tiled=True)  44 us
    all_gather x1, blocking collectives, body(): grad_pair_block = lax.all_gather(grad_pair, 'gz', axis=0, tiled=True)  20.1 us
    reduce_scatter x1, waiting for transfers between devices, body(): lax.psum_scatter(contract_last(piece, down_full), 'gz', scatter_dimension...  16.7 us
  transfers between devices with their start and end apart: 8, of which 4 were waited for; matrix products, arithmetic and copies ran while one was open for 19% of the time, Pallas kernels for 0%

commit v1 on v0

v1 whole, which is shorter than its diff:
```python
import functools
import math

import jax
import jax.numpy as jnp
from jax import lax
from jax.experimental import pallas as pl
from jax.experimental.pallas import tpu as pltpu
from jax.sharding import PartitionSpec as P

BF = jnp.bfloat16
F32 = jnp.float32
MESH_ID = pl.DeviceIdType.MESH


def dot_nn(a, b):
    return lax.dot_general(a, b, (((1,), (0,)), ((), ())), preferred_element_type=F32)


def dot_nt(a, b):
    return lax.dot_general(a, b, (((1,), (1,)), ((), ())), preferred_element_type=F32)


LAYOUT = {}
COUNT = 0
for name, size in (
    ("zh", 2), ("y", 6), ("x", 6), ("wx", 4), ("wc", 4), ("wd", 1),
    ("rh", 4), ("rp", 4), ("ag", 12), ("ox", 8), ("oy", 8), ("oz", 2),
    ("gc", 8), ("gx", 8), ("gd", 1),
):
    LAYOUT[name] = COUNT
    COUNT += size


def kernel(
    factor,
    tok_ref, cot_ref, wl_ref, wd_ref,
    mixed_ref, gtok_ref, ggate_ref, gup_ref, gdown_ref,
    acts, w, wd, zs_h, zr_h, own_h, zs_p, zr_p, own_p, mids, tok_t, hid_t,
    o_send, o_recv, o_own, y_own, y_recv, z_send, z_recv,
    gc_send, gc_recv, g_own, gx_send, gx_recv, gd_send, gd_recv,
    send, recv,
):
    gx, gy, z = lax.axis_index("gx"), lax.axis_index("gy"), lax.axis_index("gz")
    y, h = gx // 2, gx % 2
    x, c = gy // 2, gy % 2
    oc = 1 - c

    def at(dx=0, dc=0, dy=0, dh=0, dz=0):
        px, py, pz = (x + dx) % 4, (y + dy) % 4, (z + dz) % 4
        ph, pc = (h + dh) % 2, (c + dc) % 2
        return (py * 2 + ph, px * 2 + pc, pz)

    def copy(src, dst, who, name, s_off, r_off=None):
        r_off = s_off if r_off is None else r_off
        return pltpu.make_async_remote_copy(
            src_ref=src, dst_ref=dst,
            send_sem=send.at[LAYOUT[name] + s_off], recv_sem=recv.at[LAYOUT[name] + r_off],
            device_id=who, device_id_type=MESH_ID,
        )

    started = []

    def go(*args):
        cp = copy(*args)
        cp.start()
        started.append(cp)
        return cp

    peers = (
        [at(dx=k) for k in (1, 2, 3)] + [at(dy=k) for k in (1, 2, 3)]
        + [at(dz=k) for k in (1, 2, 3)] + [at(dh=1), at(dc=1)]
    )
    barrier = pltpu.get_barrier_semaphore()
    for who in peers:
        pl.semaphore_signal(barrier, inc=1, device_id=who, device_id_type=MESH_ID)
    acts[0, 0:16, :] = cot_ref[...]
    acts[1, 0:16, :] = tok_ref[...]
    wd[pl.ds(pl.multiple_of(c * 256, 256), 256), :] = wd_ref[...]
    row_own = pl.multiple_of((x * 2 + c) * 128, 128)
    w[pl.ds(row_own, 128), :] = wl_ref[x]
    pl.semaphore_wait(barrier, len(peers))

    zh = [
        go((cot_ref, tok_ref)[i], acts.at[i, pl.ds(16, 16), :], at(dh=1), "zh", i) for i in (0, 1)
    ]
    wd_slot = wd.at[pl.ds(pl.multiple_of(c * 256, 256), 256), :]
    wdc = go(wd_ref, wd_slot, at(dc=1), "wd", 0)
    wx = {}
    for r in (1, 3, 2):
        wx[r] = go(wl_ref.at[(x + r) % 4], w.at[pl.ds(row_own, 128), :], at(dx=r), "wx", r)
    wc = [go(wl_ref.at[x], w.at[pl.ds(row_own, 128), :], at(dc=1), "wc", 0)]

    def spread_y(i):
        zh[i].wait_recv()
        src = acts.at[i, pl.ds(0, 32), :]
        return [
            go(src, acts.at[i, pl.ds(32 * m, 32), :], at(dy=m), "y", i * 3 + m - 1) for m in (1, 2, 3)
        ]

    def spread_x(i, copies):
        for cp in copies:
            cp.wait_recv()
        src = acts.at[i, pl.ds(0, 128), :]
        return {
            k: go(src, acts.at[i, pl.ds(128 * k, 128), :], at(dx=k), "x", i * 3 + k - 1)
            for k in (1, 3, 2)
        }

    def z_send_block(k, src, dst, name):
        @pl.when(z != k)
        def _():
            r = (k - z + 4) % 4
            copy(src.at[k], dst.at[r], (gx, gy, k), name, k, r).start()

    def hidden_grad(k):
        def tile(j, carry):
            rows = pl.ds(pl.multiple_of(j * 256, 256), 256)
            part = dot_nt(acts[0, 128 * k:128 * (k + 1), :], wd[rows, :])
            zs_h[k, :, rows] = part.astype(BF)

            @pl.when(z == k)
            def _():
                own_h[:, rows] = part

            return carry

        lax.fori_loop(0, 2, tile, 0)
        z_send_block(k, zs_h, zr_h, "rh")

    def gate_up(k):
        def tile(j, carry):
            cols = pl.ds(pl.multiple_of(j * 256, 256), 256)
            part = dot_nn(acts[1, 128 * k:128 * (k + 1), :], w[:, cols])
            zs_p[k, :, cols] = part.astype(BF)

            @pl.when(z == k)
            def _():
                own_p[:, cols] = part

            return carry

        lax.fori_loop(0, 4, tile, 0)
        z_send_block(k, zs_p, zr_p, "rp")

    cot_y = spread_y(0)
    tok_y = spread_y(1)
    cot_x = spread_x(0, cot_y)
    wdc.wait_recv()
    hidden_grad(0)
    for r in (1, 3, 2):
        wx[r].wait_recv()
        rows = pl.ds(pl.multiple_of(((x - r + 4) % 4 * 2 + c) * 128, 128), 128)
        wc.append(go(w.at[rows, :], w.at[rows, :], at(dc=1), "wc", r))
    tok_x = spread_x(1, tok_y)
    for k in (1, 3, 2):
        cot_x[k].wait_recv()
        hidden_grad(k)
    for cp in wc:
        cp.wait_recv()
    gate_up(0)
    for k in (1, 3, 2):
        tok_x[k].wait_recv()
        gate_up(k)

    def flip(k, carry):
        rows = pl.ds(pl.multiple_of(k * 128, 128), 128)
        tok_t[:, rows] = acts[1, rows, :].T
        return carry

    lax.fori_loop(0, 4, flip, 0)

    for r in (1, 2, 3):
        copy(zs_h.at[0], zr_h.at[r], at(dz=r), "rh", 0, r).wait_recv()
        copy(zs_p.at[0], zr_p.at[r], at(dz=r), "rp", 0, r).wait_recv()

    def mix(j, carry):
        cols = pl.ds(pl.multiple_of(j * 128, 128), 128)
        upper = pl.ds(pl.multiple_of(j * 128 + 512, 128), 128)

        def total(own, got, where):
            return (
                (own[:, where] + got[1, :, where].astype(F32))
                + (got[2, :, where].astype(F32) + got[3, :, where].astype(F32))
            )

        gate = total(own_p, zr_p, cols)
        up = total(own_p, zr_p, upper)
        grad = total(own_h, zr_h, cols)
        sigma = jax.nn.sigmoid(gate)
        swish = gate * sigma
        mids[0, z, :, cols] = (grad * swish).astype(BF)
        mids[1, z, :, cols] = (grad * up * sigma * (1.0 + gate * (1.0 - sigma))).astype(BF)
        mids[2, z, :, cols] = (swish * up).astype(BF)
        return carry

    lax.fori_loop(0, 4, mix, 0)
    for m in (0, 1, 2):
        for r in (1, 3, 2):
            go(mids.at[m, z], mids.at[m, z], at(dz=r), "ag", m * 4 + r)

    def arrived(m):
        for r in (1, 2, 3):
            slot = mids.at[m, (z - r + 4) % 4]
            copy(slot, slot, at(dz=r), "ag", m * 4 + r).wait_recv()

    def whole(m):
        return mids[m].reshape(512, 512)

    def weight_grad(m):
        cps = []
        for r in (1, 3, 2, 0):
            to = (x + r) % 4
            rows = pl.ds(pl.multiple_of((to * 2 + oc) * 128, 128), 128)
            gc_send[m, r] = (dot_nn(tok_t[rows, :], whole(m)) * factor).astype(BF)
            cps.append(go(gc_send.at[m, r], gc_recv.at[m, r], at(dc=1), "gc", m * 4 + r))
        for r, cp in zip((1, 3, 2, 0), cps):
            to = (x + r) % 4
            rows = pl.ds(pl.multiple_of((to * 2 + c) * 128, 128), 128)
            mine = dot_nn(tok_t[rows, :], whole(m)) * factor
            cp.wait_recv()
            both = mine + gc_recv[m, r].astype(F32)
            if r:
                gx_send[m, r] = both.astype(BF)
                go(gx_send.at[m, r], gx_recv.at[m, r], at(dx=r), "gx", m * 4 + r)
            else:
                g_own[m] = both

    def out_block(n, k, value):
        def tile(j, carry):
            cols = pl.ds(pl.multiple_of(j * 256, 256), 256)
            part = value(cols)
            if k:
                o_send[n, k, :, cols] = part.astype(BF)
            else:
                o_own[n, :, cols] = part
            return carry

        lax.fori_loop(0, 4, tile, 0)
        if k:
            go(o_send.at[n, k], o_recv.at[n, k], at(dx=4 - k), "ox", n * 4 + k)

    arrived(0)
    weight_grad(0)
    arrived(1)
    for k in (1, 3, 2, 0):
        out_block(
            0, k,
            lambda cols, k=k: dot_nt(mids[1, k], w[cols, 0:512]) + dot_nt(mids[0, k], w[cols, 512:1024]),
        )
    weight_grad(1)
    arrived(2)
    for k in (1, 3, 2, 0):
        out_block(1, k, lambda cols, k=k: dot_nn(mids[2, k], wd[:, cols]))

    for k in range(4):
        hid_t[:, 128 * k:128 * (k + 1)] = mids[2, k].T
    theirs = pl.ds(pl.multiple_of(oc * 256, 256), 256)
    ours = pl.ds(pl.multiple_of(c * 256, 256), 256)

    def down_theirs(j, carry):
        cols = pl.ds(pl.multiple_of(j * 256, 256), 256)
        gd_send[:, cols] = (dot_nn(hid_t[theirs, :], acts[0, :, cols]) * factor).astype(BF)
        return carry

    lax.fori_loop(0, 4, down_theirs, 0)
    gd = go(gd_send, gd_recv, at(dc=1), "gd", 0)

    def down_ours(j, carry):
        cols = pl.ds(pl.multiple_of(j * 256, 256), 256)
        gdown_ref[:, cols] = dot_nn(hid_t[ours, :], acts[0, :, cols]) * factor
        return carry

    lax.fori_loop(0, 4, down_ours, 0)

    oy = {}
    for n in (0, 1):
        for k in (1, 2, 3):
            copy(o_send.at[n, k], o_recv.at[n, k], at(dx=4 - k), "ox", n * 4 + k).wait_recv()
        y_own[n] = (o_own[n] + o_recv[n, 1].astype(F32)) + (
            o_recv[n, 2].astype(F32) + o_recv[n, 3].astype(F32)
        )
        for m in (1, 3, 2):
            oy[n, m] = go(
                y_own.at[n, pl.ds(32 * m, 32), :], y_recv.at[n, m], at(dy=4 - m), "oy", n * 4 + m
            )
    oz = []
    for n in (0, 1):
        for m in (1, 2, 3):
            oy[n, m].wait_recv()
        z_send[n] = (y_own[n, 0:32, :] + y_recv[n, 1]) + (y_recv[n, 2] + y_recv[n, 3])
        oz.append(go(z_send.at[n, pl.ds(16, 16), :], z_recv.at[n], at(dh=1), "oz", n))

    gd.wait_recv()
    gdown_ref[...] += gd_recv[...].astype(F32)
    for m, out in ((0, gup_ref), (1, ggate_ref)):
        for r in (1, 2, 3):
            copy(gx_send.at[m, r], gx_recv.at[m, r], at(dx=r), "gx", m * 4 + r).wait_recv()
            cols = pl.ds(pl.multiple_of((x - r + 4) % 4 * 512, 512), 512)
            out[:, cols] = gx_recv[m, r].astype(F32)
        out[:, pl.ds(pl.multiple_of(x * 512, 512), 512)] = g_own[m]
    for n, out in ((0, gtok_ref), (1, mixed_ref)):
        oz[n].wait_recv()
        out[...] = (z_send[n, 0:16, :] + z_recv[n]).astype(BF)

    for cp in started:
        cp.wait_send()
    for k in range(4):
        @pl.when(z != k)
        def _():
            copy(zs_h.at[k], zr_h.at[1], (gx, gy, k), "rh", k, 1).wait_send()
            copy(zs_p.at[k], zr_p.at[1], (gx, gy, k), "rp", k, 1).wait_send()


def body(tokens, gate_weight, up_weight, down_weight, cotangent):
    unit = gate_weight.shape[1] // 8
    gap = 256 - unit

    def widen(a):
        return jnp.pad(a.reshape(128, 8, unit), ((0, 0), (0, 0), (0, gap))).reshape(128, 4, 512)

    wl = jnp.concatenate([widen(gate_weight), widen(up_weight)], axis=2).transpose(1, 0, 2)
    wd = jnp.pad(down_weight, ((0, gap), (0, 0)))
    vmem = pl.BlockSpec(memory_space=pltpu.VMEM)
    factor = 1.0 / math.sqrt(1024)
    mixed, gtok, ggate, gup, gdown = pl.pallas_call(
        functools.partial(kernel, factor),
        name="swiglu",
        out_shape=(
            jax.ShapeDtypeStruct((16, 1024), BF),
            jax.ShapeDtypeStruct((16, 1024), BF),
            jax.ShapeDtypeStruct((128, 2048), F32),
            jax.ShapeDtypeStruct((128, 2048), F32),
            jax.ShapeDtypeStruct((256, 1024), F32),
        ),
        in_specs=[vmem] * 4,
        out_specs=[vmem] * 5,
        scratch_shapes=[
            pltpu.VMEM((2, 512, 1024), BF),
            pltpu.VMEM((1024, 1024), BF),
            pltpu.VMEM((512, 1024), BF),
            pltpu.VMEM((4, 128, 512), BF),
            pltpu.VMEM((4, 128, 512), BF),
            pltpu.VMEM((128, 512), F32),
            pltpu.VMEM((4, 128, 1024), BF),
            pltpu.VMEM((4, 128, 1024), BF),
            pltpu.VMEM((128, 1024), F32),
            pltpu.VMEM((3, 4, 128, 512), BF),
            pltpu.VMEM((1024, 512), BF),
            pltpu.VMEM((512, 512), BF),
            pltpu.VMEM((2, 4, 128, 1024), BF),
            pltpu.VMEM((2, 4, 128, 1024), BF),
            pltpu.VMEM((2, 128, 1024), F32),
            pltpu.VMEM((2, 128, 1024), F32),
            pltpu.VMEM((2, 4, 32, 1024), F32),
            pltpu.VMEM((2, 32, 1024), F32),
            pltpu.VMEM((2, 16, 1024), F32),
            pltpu.VMEM((2, 4, 128, 512), BF),
            pltpu.VMEM((2, 4, 128, 512), BF),
            pltpu.VMEM((2, 128, 512), F32),
            pltpu.VMEM((2, 4, 128, 512), BF),
            pltpu.VMEM((2, 4, 128, 512), BF),
            pltpu.VMEM((256, 1024), BF),
            pltpu.VMEM((256, 1024), BF),
            pltpu.SemaphoreType.DMA((COUNT,)),
            pltpu.SemaphoreType.DMA((COUNT,)),
        ],
        compiler_params=pltpu.CompilerParams(
            collective_id=1, has_side_effects=True, vmem_limit_bytes=48 << 20
        ),
    )(tokens, cotangent, wl, wd)

    def narrow(a):
        return jnp.concatenate([a[:, 256 * j:256 * j + unit] for j in range(8)], axis=1)

    return mixed, gtok, narrow(ggate), narrow(gup), gdown[:unit]


def solution(mesh):
    in_specs = (
        P(("gy", "gx"), "gz"),
        P(("gz", "gy"), "gx"),
        P(("gz", "gy"), "gx"),
        P(("gx", "gy"), "gz"),
        P(("gy", "gx"), "gz"),
    )
    out_specs = (
        P(("gy", "gx"), "gz"),
        P(("gy", "gx"), "gz"),
        P(("gz", "gy"), "gx"),
        P(("gz", "gy"), "gx"),
        P(("gx", "gy"), "gz"),
    )
    return jax.shard_map(body, mesh=mesh, in_specs=in_specs, out_specs=out_specs, check_vma=False)
```

time: 470 us -> 157 us (0.33)
  the two profiles are of different devices: /device:TPU:40 before, /device:TPU:2 now
where the time goes in v1:
time: 157 us
  Pallas kernels  147 us (94%)
  local copies, waits for them, and re-layouts  9.27 us (6%)
    pallas_call x1, Pallas kernels, body(): pl.pallas_call(functools.partial(kernel, factor), name='swiglu', out_shap...  147 us
    unnamed x12, local copies, waits for them, and re-layouts  5.35 us

profile of v1, /device:TPU:2, one launch (start us, length us, event | category | flops | bytes accessed | tf_op | source)
XLA Modules:
  0.0 157.2 jit_solution(16152609091897807766)
XLA Ops:
  0.6 1.2 reshape.22
  1.8 0.0 copy-start.3
  1.9 0.2 copy.12
  2.1 0.7 copy-done.3
  2.8 0.1 reshape.24
  3.0 0.2 copy.13
  3.3 0.0 copy-start.2
  3.3 0.0 copy-start
  3.3 0.0 copy-start.1
  3.3 0.1 maximum_bitcast_fusion.wl_ref
  3.4 0.8 copy-done.2
  4.3 0.0 copy-done
  4.3 0.0 copy-done.1
  4.4 147.1 %swiglu.1 = (bf16[16,1024]{1,0:T(8,128)(2,1)S(1)}, bf16[16,1024]{1,0:T(8,128)(2,1)S(1)}, f32[128,2048]{1,0:T(8,128)S(1)}, f32[128,2048]{1,0:T(8,128)S(1)}, f32[256,1024]{1,0:T(8,128)S(1)}) custom-call(bf16[16,1024]{1,0:T(8,128)(2,1)S(1)} %copy-done, bf16[16,1024]{1,0:T(8,128)(2,1)S(1)} %copy-done.1, bf16[4,128,1024]{2,1,0:T(8,128)(2,1)S(1)} %maximum_bitcast_fusion.wl_ref, ...), custom_call_target="tpu_custom_call" | custom-call | tf_op jit(solution)/shard_map/swiglu/pallas_call | solution.py:326
  151.4 1.0 slice.67
  152.5 0.2 fusion
  152.7 0.4 concatenate.11
  153.1 1.3 copy.15
  154.4 0.4 concatenate.10
  154.8 1.3 copy.14
  156.0 0.6 copy.18
  156.6 0.6 copy.19
  (3 shorter events, 0.1 us)
Async XLA Ops:
  1.8 1.0 copy-start.3
  3.3 1.0 copy-start.2
  3.3 1.1 copy-start
  3.3 1.1 copy-start.1

commit v2 on v1

v2 whole, which is shorter than its diff:
```python
import functools
import math

import jax
import jax.numpy as jnp
from jax import lax
from jax.experimental import pallas as pl
from jax.experimental.pallas import tpu as pltpu
from jax.sharding import PartitionSpec as P

BF = jnp.bfloat16
F32 = jnp.float32
MESH_ID = pl.DeviceIdType.MESH
UNIT = 231


def dot_nn(a, b):
    return lax.dot_general(a, b, (((1,), (0,)), ((), ())), preferred_element_type=F32)


def dot_nt(a, b):
    return lax.dot_general(a, b, (((1,), (1,)), ((), ())), preferred_element_type=F32)


LAYOUT = {}
COUNT = 0
for name, size in (
    ("zh", 2), ("y", 6), ("x", 6), ("wx", 4), ("wc", 4), ("wd", 1),
    ("rh", 16), ("rp", 16), ("lh", 4), ("lp", 4), ("ag", 16), ("af", 4),
    ("ox", 8), ("oy", 8), ("oz", 2), ("gc", 2), ("gx", 8), ("gd", 1),
):
    LAYOUT[name] = COUNT
    COUNT += size


def kernel(
    factor,
    tok_ref, cot_ref, gw_ref, uw_ref, wd_ref,
    mixed_ref, gtok_ref, ggate_ref, gup_ref, gdown_ref,
    acts, w_loc, w, wd, parts, zs_h, zr_h, rl_h, zs_p, zr_p, rl_p, mids, tok_t, hid_t,
    o_send, o_recv, o_own, y_own, y_recv, z_send, z_recv,
    gc_send, gc_recv, g_acc, gx_send, gx_recv, gd_send, gd_recv,
    send, recv,
):
    gx, gy, z = lax.axis_index("gx"), lax.axis_index("gy"), lax.axis_index("gz")
    y, h = gx // 2, gx % 2
    x, c = gy // 2, gy % 2
    oc = 1 - c

    def at(dx=0, dc=0, dy=0, dh=0, dz=0):
        px, py, pz = (x + dx) % 4, (y + dy) % 4, (z + dz) % 4
        ph, pc = (h + dh) % 2, (c + dc) % 2
        return (py * 2 + ph, px * 2 + pc, pz)

    def copy(src, dst, who, name, s_off, r_off=None):
        r_off = s_off if r_off is None else r_off
        return pltpu.make_async_remote_copy(
            src_ref=src, dst_ref=dst,
            send_sem=send.at[LAYOUT[name] + s_off], recv_sem=recv.at[LAYOUT[name] + r_off],
            device_id=who, device_id_type=MESH_ID,
        )

    started = []
    pending = []

    def go(*args):
        cp = copy(*args)
        cp.start()
        started.append(cp)
        return cp

    def go_if(cond, *args):
        @pl.when(cond)
        def _():
            copy(*args).start()

        pending.append((cond, args))

    def wait_if(cond, *args):
        @pl.when(cond)
        def _():
            copy(*args).wait_recv()

    inner = (z == 1) | (z == 2)
    via = 1 + z // 3
    far = 3 - z
    relay_to = 3 * ((2 - z + 4) % 4 % 2)

    peers = (
        [at(dx=k) for k in (1, 2, 3)] + [at(dy=k) for k in (1, 2, 3)]
        + [at(dz=k) for k in (1, 2, 3)] + [at(dh=1), at(dc=1)]
    )
    barrier = pltpu.get_barrier_semaphore()
    for who in peers:
        pl.semaphore_signal(barrier, inc=1, device_id=who, device_id_type=MESH_ID)
    acts[0, 0:16, :] = cot_ref[...]
    acts[1, 0:16, :] = tok_ref[...]
    wd_rows = pl.ds(pl.multiple_of(c * 256, 256), 256)
    wd[wd_rows, :] = wd_ref[...]
    zeros = jnp.zeros((128, 256), BF)
    for n, ref in ((0, uw_ref), (1, gw_ref)):
        for j in range(8):
            base = n * 512 + (j % 2) * 256
            w_loc[j // 2, :, base:base + 256] = zeros
            w_loc[j // 2, :, base:base + UNIT] = ref[:, UNIT * j:UNIT * (j + 1)]
    row_own = pl.multiple_of((x * 2 + c) * 128, 128)
    w_rows = pl.ds(row_own, 128)
    w[w_rows, :] = w_loc[x]
    pl.semaphore_wait(barrier, len(peers))

    zh = [
        go((cot_ref, tok_ref)[i], acts.at[i, pl.ds(16, 16), :], at(dh=1), "zh", i) for i in (0, 1)
    ]
    wdc = go(wd_ref, wd.at[wd_rows, :], at(dc=1), "wd", 0)
    wx = {}
    for r in (1, 3, 2):
        wx[r] = go(w_loc.at[(x + r) % 4], w.at[w_rows, :], at(dx=r), "wx", r)
    wc = [go(w_loc.at[x], w.at[w_rows, :], at(dc=1), "wc", 0)]

    @pl.when(jnp.logical_not(inner))
    def _():
        zr_h[:, far] = jnp.zeros((4, 32, 512), BF)
        zr_p[:, far] = jnp.zeros((4, 32, 1024), BF)

    def spread_y(i):
        zh[i].wait_recv()
        src = acts.at[i, pl.ds(0, 32), :]
        return [
            go(src, acts.at[i, pl.ds(32 * m, 32), :], at(dy=m), "y", i * 3 + m - 1) for m in (1, 3, 2)
        ]

    def spread_x(i, copies):
        for cp in copies:
            cp.wait_recv()
        src = acts.at[i, pl.ds(0, 128), :]
        return {
            k: go(src, acts.at[i, pl.ds(128 * k, 128), :], at(dx=k), "x", i * 3 + k - 1)
            for k in (1, 3, 2)
        }

    def scatter(k, src, dst, relay, name, relay_name):
        for m in range(4):
            rows = src.at[k, pl.ds(32 * m, 32)]
            direct = (z == 1) if m == 0 else (z == 2) if m == 3 else (z != m)
            go_if(direct, rows, dst.at[k, z], (gx, gy, m), name, k * 4 + m, k * 4 + z)
            if m in (0, 3):
                go_if(z == 3 - m, rows, relay.at[k], (gx, gy, via), relay_name, k)

    def hidden_grad(k):
        def tile(j, carry):
            rows = pl.ds(pl.multiple_of(j * 256, 256), 256)
            part = dot_nt(acts[0, 128 * k:128 * (k + 1), :], wd[rows, :])
            zs_h[k, :, rows] = part.astype(BF)
            parts[k, :, pl.ds(pl.multiple_of(j * 256 + 1024, 256), 256)] = part
            return carry

        lax.fori_loop(0, 2, tile, 0)
        scatter(k, zs_h, zr_h, rl_h, "rh", "lh")

    def gate_up(k):
        def tile(j, carry):
            cols = pl.ds(pl.multiple_of(j * 256, 256), 256)
            part = dot_nn(acts[1, 128 * k:128 * (k + 1), :], w[:, cols])
            zs_p[k, :, cols] = part.astype(BF)
            parts[k, :, cols] = part
            return carry

        lax.fori_loop(0, 4, tile, 0)
        scatter(k, zs_p, zr_p, rl_p, "rp", "lp")

    def relay(k):
        rows = pl.ds(pl.multiple_of(relay_to * 32, 32), 32)

        @pl.when(inner)
        def _():
            copy(rl_h.at[k], rl_h.at[k], (gx, gy, 3 - relay_to), "lh", k).wait_recv()
            zs_h[k, rows, :] = (parts[k, rows, 1024:1536] + rl_h[k].astype(F32)).astype(BF)
            copy(rl_p.at[k], rl_p.at[k], (gx, gy, 3 - relay_to), "lp", k).wait_recv()
            zs_p[k, rows, :] = (parts[k, rows, 0:1024] + rl_p[k].astype(F32)).astype(BF)

        for m in (0, 3):
            sel = z == (2 if m == 0 else 1)
            piece = pl.ds(32 * m, 32)
            go_if(sel, zs_h.at[k, piece], zr_h.at[k, z], (gx, gy, m), "rh", k * 4 + m, k * 4 + z)
            go_if(sel, zs_p.at[k, piece], zr_p.at[k, z], (gx, gy, m), "rp", k * 4 + m, k * 4 + z)

    def mix(k):
        for s in range(4):
            cond = (z != s) & (z != 3 - s) if s in (0, 3) else z != s
            wait_if(cond, zs_h.at[k, pl.ds(0, 32)], zr_h.at[k, s], (gx, gy, s), "rh", k * 4 + s)
            wait_if(cond, zs_p.at[k, pl.ds(0, 32)], zr_p.at[k, s], (gx, gy, s), "rp", k * 4 + s)
        mine = pl.ds(pl.multiple_of(z * 32, 32), 32)
        out = pl.ds(pl.multiple_of(z * 32 + 128 * k, 32), 32)

        def tile(j, carry):
            def total(got, off, skip):
                here = pl.ds(pl.multiple_of(j * 128 + off, 128), 128)
                mid = pl.ds(pl.multiple_of(j * 128 + off + skip, 128), 128)
                return (
                    (parts[k, mine, mid] + got[k, (z + 1) % 4, :, here].astype(F32))
                    + (got[k, (z + 2) % 4, :, here].astype(F32) + got[k, (z + 3) % 4, :, here].astype(F32))
                )

            up = total(zr_p, 0, 0)
            gate = total(zr_p, 512, 0)
            grad = total(zr_h, 0, 1024)
            sigma = jax.nn.sigmoid(gate)
            swish = gate * sigma

            def put(n, value):
                mids[out, pl.ds(pl.multiple_of(j * 128 + 512 * n, 128), 128)] = value.astype(BF)

            put(0, grad * swish)
            put(1, grad * up * sigma * (1.0 + gate * (1.0 - sigma)))
            put(2, swish * up)
            return carry

        lax.fori_loop(0, 4, tile, 0)
        block = mids.at[out, :]
        for m in range(4):
            cond = (z != m) & (z != 3 - m) if m in (0, 3) else z != m
            go_if(cond, block, block, (gx, gy, m), "ag", k * 4 + m, k * 4 + z)

    def forward(k):
        for m in (0, 3):
            sel = z == (1 if m == 0 else 2)
            block = mids.at[pl.ds(128 * k + 32 * (3 - m), 32), :]
            wait_if(sel, block, block, (gx, gy, 3 - m), "ag", k * 4 + 3 - m)
            go_if(sel, block, block, (gx, gy, m), "af", k, k * 4 - LAYOUT["af"] + LAYOUT["ag"] + 3 - m)

    def arrived(k):
        for s in range(4):
            cond = z != s
            if s == 0:
                cond = cond & (z != 2)
            if s == 3:
                cond = cond & (z != 1)
            block = mids.at[pl.ds(128 * k + 32 * s, 32), :]
            wait_if(cond, block, block, (gx, gy, s), "ag", k * 4 + s)

    def out_block(n, k):
        slot = pl.ds(128 * k, 128)

        def tile(j, carry):
            cols = pl.ds(pl.multiple_of(j * 256, 256), 256)
            if n == 0:
                part = dot_nt(mids[slot, 0:1024], w[cols, :])
            else:
                part = dot_nn(mids[slot, 1024:1536], wd[:, cols])
            if k:
                o_send[n, k, :, cols] = part.astype(BF)
            else:
                o_own[n, :, cols] = part
            return carry

        lax.fori_loop(0, 4, tile, 0)
        if k:
            go(o_send.at[n, k], o_recv.at[n, k], at(dx=4 - k), "ox", n * 4 + k)

    def project(k):
        arrived(k)
        out_block(0, k)
        out_block(1, k)

    cot_y = spread_y(0)
    tok_y = spread_y(1)
    cot_x = spread_x(0, cot_y)
    wdc.wait_recv()
    hidden_grad(0)
    for r in (1, 3, 2):
        wx[r].wait_recv()
        rows = pl.ds(pl.multiple_of(((x - r + 4) % 4 * 2 + c) * 128, 128), 128)
        wc.append(go(w.at[rows, :], w.at[rows, :], at(dc=1), "wc", r))
    tok_x = spread_x(1, tok_y)
    for cp in wc:
        cp.wait_recv()
    gate_up(0)
    for k in (1, 3, 2):
        cot_x[k].wait_recv()
        hidden_grad(k)
    relay(0)
    mix(0)
    tok_x[1].wait_recv()
    gate_up(1)
    forward(0)
    tok_x[3].wait_recv()
    gate_up(3)
    relay(1)
    mix(1)
    tok_x[2].wait_recv()
    gate_up(2)
    relay(3)
    forward(1)
    project(0)
    mix(3)
    relay(2)
    forward(3)
    project(1)
    mix(2)

    for j in range(8):
        tok_t[j % 2, 128 * (j // 2):128 * (j // 2 + 1), :] = acts[1, :, 128 * j:128 * (j + 1)].T

    forward(2)
    project(3)
    project(2)

    def grads(n, mine):
        side = c if mine else oc

        def tile(j, carry):
            cols = pl.ds(pl.multiple_of(j * 256, 256), 256)
            source = pl.ds(pl.multiple_of(j * 256 + 512 * n, 256), 256)
            part = dot_nn(tok_t[side], mids[:, source]) * factor
            if mine:
                g_acc[n, :, cols] = part
            else:
                gc_send[n, :, cols] = part.astype(BF)
            return carry

        lax.fori_loop(0, 2, tile, 0)

    def spread_grads(n, cp):
        cp.wait_recv()
        for r in (1, 3, 2):
            to = (x + r) % 4
            rows = pl.ds(pl.multiple_of(to * 128, 128), 128)
            gx_send[n, r] = (g_acc[n, rows, :] + gc_recv[n, rows, :].astype(F32)).astype(BF)
            go(gx_send.at[n, r], gx_recv.at[n, x], at(dx=r), "gx", n * 4 + r)
        rows = pl.ds(pl.multiple_of(x * 128, 128), 128)
        g_acc[n, rows, :] = g_acc[n, rows, :] + gc_recv[n, rows, :].astype(F32)

    grads(0, False)
    gc0 = go(gc_send.at[0], gc_recv.at[0], at(dc=1), "gc", 0)
    grads(1, False)
    gc1 = go(gc_send.at[1], gc_recv.at[1], at(dc=1), "gc", 1)
    grads(0, True)
    spread_grads(0, gc0)
    grads(1, True)
    spread_grads(1, gc1)

    for k in range(4):
        hid_t[:, 128 * k:128 * (k + 1)] = mids[128 * k:128 * (k + 1), 1024:1536].T
    theirs = pl.ds(pl.multiple_of(oc * 256, 256), 256)

    def down_theirs(j, carry):
        cols = pl.ds(pl.multiple_of(j * 256, 256), 256)
        gd_send[:, cols] = (dot_nn(hid_t[theirs, :], acts[0, :, cols]) * factor).astype(BF)
        return carry

    lax.fori_loop(0, 4, down_theirs, 0)
    gd = go(gd_send, gd_recv, at(dc=1), "gd", 0)

    oy = {}
    for n in (0, 1):
        for k in (1, 2, 3):
            copy(o_send.at[n, k], o_recv.at[n, k], at(dx=4 - k), "ox", n * 4 + k).wait_recv()
        y_own[n] = (o_own[n] + o_recv[n, 1].astype(F32)) + (
            o_recv[n, 2].astype(F32) + o_recv[n, 3].astype(F32)
        )
        for m in (1, 3, 2):
            oy[n, m] = go(
                y_own.at[n, pl.ds(32 * m, 32), :], y_recv.at[n, m], at(dy=4 - m), "oy", n * 4 + m
            )

    def down_ours(j, carry):
        cols = pl.ds(pl.multiple_of(j * 256, 256), 256)
        gdown_ref[:, cols] = dot_nn(hid_t[wd_rows, :], acts[0, :, cols]) * factor
        return carry

    lax.fori_loop(0, 4, down_ours, 0)
    gd.wait_recv()
    gdown_ref[...] += gd_recv[...].astype(F32)

    oz = []
    for n in (0, 1):
        for m in (1, 2, 3):
            oy[n, m].wait_recv()
        z_send[n] = (y_own[n, 0:32, :] + y_recv[n, 1]) + (y_recv[n, 2] + y_recv[n, 3])
        oz.append(go(z_send.at[n, pl.ds(16, 16), :], z_recv.at[n], at(dh=1), "oz", n))

    for n, out in ((0, gup_ref), (1, ggate_ref)):
        for r in (1, 2, 3):
            slot = (x - r + 4) % 4
            copy(gx_send.at[n, r], gx_recv.at[n, slot], at(dx=r), "gx", n * 4 + r).wait_recv()
        rows = pl.ds(pl.multiple_of(x * 128, 128), 128)
        for p in range(4):
            for j in (0, 1):
                cols = slice(256 * j, 256 * j + UNIT)
                to = slice(UNIT * (2 * p + j), UNIT * (2 * p + j + 1))

                @pl.when(x == p)
                def _():
                    out[:, to] = g_acc[n, rows, cols]

                @pl.when(x != p)
                def _():
                    out[:, to] = gx_recv[n, p, :, cols].astype(F32)

    for n, out in ((0, gtok_ref), (1, mixed_ref)):
        oz[n].wait_recv()
        out[...] = (z_send[n, 0:16, :] + z_recv[n]).astype(BF)

    for cp in started:
        cp.wait_send()
    for cond, args in pending:
        @pl.when(cond)
        def _():
            copy(*args).wait_send()


def body(tokens, gate_weight, up_weight, down_weight, cotangent):
    wd = jnp.pad(down_weight, ((0, 256 - UNIT), (0, 0)))
    vmem = pl.BlockSpec(memory_space=pltpu.VMEM)
    factor = 1.0 / math.sqrt(1024)
    mixed, gtok, ggate, gup, gdown = pl.pallas_call(
        functools.partial(kernel, factor),
        name="swiglu",
        out_shape=(
            jax.ShapeDtypeStruct((16, 1024), BF),
            jax.ShapeDtypeStruct((16, 1024), BF),
            jax.ShapeDtypeStruct((128, 1848), F32),
            jax.ShapeDtypeStruct((128, 1848), F32),
            jax.ShapeDtypeStruct((256, 1024), F32),
        ),
        in_specs=[vmem] * 5,
        out_specs=[vmem] * 5,
        scratch_shapes=[
            pltpu.VMEM((2, 512, 1024), BF),
            pltpu.VMEM((4, 128, 1024), BF),
            pltpu.VMEM((1024, 1024), BF),
            pltpu.VMEM((512, 1024), BF),
            pltpu.VMEM((4, 128, 1536), F32),
            pltpu.VMEM((4, 128, 512), BF),
            pltpu.VMEM((4, 4, 32, 512), BF),
            pltpu.VMEM((4, 32, 512), BF),
            pltpu.VMEM((4, 128, 1024), BF),
            pltpu.VMEM((4, 4, 32, 1024), BF),
            pltpu.VMEM((4, 32, 1024), BF),
            pltpu.VMEM((512, 1536), BF),
            pltpu.VMEM((2, 512, 512), BF),
            pltpu.VMEM((512, 512), BF),
            pltpu.VMEM((2, 4, 128, 1024), BF),
            pltpu.VMEM((2, 4, 128, 1024), BF),
            pltpu.VMEM((2, 128, 1024), F32),
            pltpu.VMEM((2, 128, 1024), F32),
            pltpu.VMEM((2, 4, 32, 1024), F32),
            pltpu.VMEM((2, 32, 1024), F32),
            pltpu.VMEM((2, 16, 1024), F32),
            pltpu.VMEM((2, 512, 512), BF),
            pltpu.VMEM((2, 512, 512), BF),
            pltpu.VMEM((2, 512, 512), F32),
            pltpu.VMEM((2, 4, 128, 512), BF),
            pltpu.VMEM((2, 4, 128, 512), BF),
            pltpu.VMEM((256, 1024), BF),
            pltpu.VMEM((256, 1024), BF),
            pltpu.SemaphoreType.DMA((COUNT,)),
            pltpu.SemaphoreType.DMA((COUNT,)),
        ],
        compiler_params=pltpu.CompilerParams(
            collective_id=1, has_side_effects=True, vmem_limit_bytes=48 << 20
        ),
    )(tokens, cotangent, gate_weight, up_weight, wd)
    return mixed, gtok, ggate, gup, gdown[:UNIT]


def solution(mesh):
    in_specs = (
        P(("gy", "gx"), "gz"),
        P(("gz", "gy"), "gx"),
        P(("gz", "gy"), "gx"),
        P(("gx", "gy"), "gz"),
        P(("gy", "gx"), "gz"),
    )
    out_specs = (
        P(("gy", "gx"), "gz"),
        P(("gy", "gx"), "gz"),
        P(("gz", "gy"), "gx"),
        P(("gz", "gy"), "gx"),
        P(("gx", "gy"), "gz"),
    )
    return jax.shard_map(body, mesh=mesh, in_specs=in_specs, out_specs=out_specs, check_vma=False)
```

time: 157 us -> 130 us (0.83)
  the two profiles are of different devices: /device:TPU:2 before, /device:TPU:40 now
where the time goes in v2:
time: 130 us; the launch traced here: 129 us
  Pallas kernels  119 us (92%)
  local copies, waits for them, and re-layouts  8.8 us (7%)
    pallas_call x1, Pallas kernels, body(): pl.pallas_call(functools.partial(kernel, factor), name='swiglu', out_shap...  119 us
    unnamed x18, local copies, waits for them, and re-layouts  7.76 us

profile of v2, /device:TPU:40, one launch (start us, length us, event | category | flops | bytes accessed | tf_op | source)
XLA Modules:
  0.0 129.0 jit_solution(9699827154947245996)
XLA Ops:
  0.6 0.0 copy-start.5
  0.6 1.3 %copy.10.gw_ref = bf16[128,1848]{1,0:T(8,128)(2,1)S(1)} copy(bf16[128,1848]{0,1:T(8,128)(2,1)} %param.6) | data formatting | bytes 946176 | tf_op args[1]
  2.0 0.0 copy-done.5
  2.0 0.0 copy-start.4
  2.0 0.3 copy.11.uw_ref
  2.2 0.8 copy-done.4
  3.0 0.0 copy-start.2
  3.0 0.0 copy-start.3
  3.1 0.7 copy-done.2
  3.8 0.0 copy-done.3
  3.8 119.5 %swiglu.1 = (bf16[16,1024]{1,0:T(8,128)(2,1)S(1)}, bf16[16,1024]{1,0:T(8,128)(2,1)S(1)}, f32[128,1848]{1,0:T(8,128)S(1)}, f32[128,1848]{1,0:T(8,128)S(1)}, f32[256,1024]{1,0:T(8,128)S(1)}) custom-call(bf16[16,1024]{1,0:T(8,128)(2,1)S(1)} %copy-done.2, bf16[16,1024]{1,0:T(8,128)(2,1)S(1)} %copy-done.3, bf16[128,1848]{1,0:T(8,128)(2,1)S(1)} %copy.10.gw_ref, ...), custom_call_target="tpu_custom_call" | custom-call | tf_op jit(solution)/shard_map/swiglu/pallas_call | solution.py:416
  123.3 0.0 copy-start
  123.3 1.0 copy-done
  124.2 1.2 copy.12
  125.5 0.0 copy-start.1
  125.5 1.2 copy.13
  126.7 0.0 copy-done.1
  126.7 1.0 slice.3
  127.7 0.6 copy.16
  128.3 0.6 copy.17
  (1 shorter events, 0.0 us)
Async XLA Ops:
  0.6 1.3 %copy-start.5 = (bf16[128,1848]{0,1:T(8,128)(2,1)S(1)}, bf16[128,1848]{0,1:T(8,128)(2,1)}, u32[]{:S(2)}) copy-start(bf16[128,1848]{0,1:T(8,128)(2,1)} %param.7) | copy-start | bytes 1419268
  2.0 1.0 copy-start.4
  3.0 0.8 copy-start.2
  3.0 0.8 copy-start.3
  123.3 1.0 copy-start
  125.5 1.3 copy-start.1

commit v3 on v2

v3 whole, which is shorter than its diff:
```python
import functools
import math

import jax
import jax.numpy as jnp
from jax import lax
from jax.experimental import pallas as pl
from jax.experimental.pallas import tpu as pltpu
from jax.sharding import PartitionSpec as P

BF = jnp.bfloat16
F32 = jnp.float32
ORDER = "H1 P1 R0 H3 P3 D0 H2 P2 R1 R3 F0 D1 R2 D3 F1 G0 D2 F3 G1 F2 G3 G2"
MESH_ID = pl.DeviceIdType.MESH
UNIT = 231


def dot_nn(a, b):
    return lax.dot_general(a, b, (((1,), (0,)), ((), ())), preferred_element_type=F32)


def dot_nt(a, b):
    return lax.dot_general(a, b, (((1,), (1,)), ((), ())), preferred_element_type=F32)


LAYOUT = {}
COUNT = 0
for name, size in (
    ("zh", 2), ("y", 6), ("x", 6), ("x1", 6), ("y2", 6), ("wx", 4), ("wc", 4), ("wd", 1),
    ("rh", 16), ("rp", 16), ("lh", 4), ("lp", 4), ("ag", 16), ("af", 4),
    ("ox", 8), ("oy", 8), ("oz", 2), ("py", 32), ("px", 8), ("gc", 4), ("gx", 4), ("gd", 1),
):
    LAYOUT[name] = COUNT
    COUNT += size


def kernel(
    factor,
    tok_ref, cot_ref, gw_ref, uw_ref, wd_ref,
    mixed_ref, gtok_ref, ggate_ref, gup_ref, gdown_ref,
    acts, w_loc, w, wd, parts, zs_h, zr_h, rl_h, zs_p, zr_p, rl_p, mids, mids_t, tok_in, cot_in, wd_in, wd_own,
    o_send, o_recv, o_own, p_own, p_recv, p_sum, px_recv, y_own, y_recv, z_send, z_recv,
    gc_send, gc_recv, g_acc, g_out, gx_send, gx_recv, gd_send, gd_recv, gd_own,
    send, recv, local,
):
    gx, gy, z = lax.axis_index("gx"), lax.axis_index("gy"), lax.axis_index("gz")
    y, h = gx // 2, gx % 2
    x, c = gy // 2, gy % 2
    oc = 1 - c

    def at(dx=0, dc=0, dy=0, dh=0, dz=0):
        px, py, pz = (x + dx) % 4, (y + dy) % 4, (z + dz) % 4
        ph, pc = (h + dh) % 2, (c + dc) % 2
        return (py * 2 + ph, px * 2 + pc, pz)

    def copy(src, dst, who, name, s_off, r_off=None):
        r_off = s_off if r_off is None else r_off
        return pltpu.make_async_remote_copy(
            src_ref=src, dst_ref=dst,
            send_sem=send.at[LAYOUT[name] + s_off], recv_sem=recv.at[LAYOUT[name] + r_off],
            device_id=who, device_id_type=MESH_ID,
        )

    started = []
    pending = []

    def go(*args):
        cp = copy(*args)
        cp.start()
        started.append(cp)
        return cp

    def go_if(cond, *args):
        @pl.when(cond)
        def _():
            copy(*args).start()

        pending.append((cond, args))

    def wait_if(cond, *args):
        @pl.when(cond)
        def _():
            copy(*args).wait_recv()

    inner = (z == 1) | (z == 2)
    via = 1 + z // 3
    far = 3 - z
    relay_to = 3 * ((2 - z + 4) % 4 % 2)

    peers = (
        [at(dx=k) for k in (1, 2, 3)] + [at(dy=k) for k in (1, 2, 3)]
        + [at(dz=k) for k in (1, 2, 3)] + [at(dh=1), at(dc=1)]
    )
    loads = [
        pltpu.make_async_copy(src, dst, local.at[i])
        for i, (src, dst) in enumerate(((cot_ref, cot_in), (tok_ref, tok_in), (wd_ref, wd_in)))
    ]
    for load in loads:
        load.start()
    barrier = pltpu.get_barrier_semaphore()
    for who in peers:
        pl.semaphore_signal(barrier, inc=1, device_id=who, device_id_type=MESH_ID)
    zeros = jnp.zeros((128, 256), BF)
    for n, ref in ((0, uw_ref), (1, gw_ref)):
        for j in range(8):
            base = n * 512 + (j % 2) * 256
            w_loc[j // 2, :, base:base + 256] = zeros
            w_loc[j // 2, :, base:base + UNIT] = ref[:, UNIT * j:UNIT * (j + 1)]
    row_own = pl.multiple_of((x * 2 + c) * 128, 128)
    w_rows = pl.ds(row_own, 128)
    w[w_rows, :] = w_loc[x]
    for load in loads:
        load.wait()
    acts[0, 0, 0, 0:16, :] = cot_in[...]
    acts[1, 0, 0, 0:16, :] = tok_in[...]
    wd_rows = pl.ds(pl.multiple_of(c * 256, 256), 256)
    wd_own[224:256, :] = jnp.zeros((32, 1024), BF)
    wd_own[0:UNIT, :] = wd_in[...]
    wd[wd_rows, :] = wd_own[...]
    pl.semaphore_wait(barrier, len(peers))

    zh = [
        go((cot_in, tok_in)[i], acts.at[i, 0, 0, pl.ds(16, 16), :], at(dh=1), "zh", i) for i in (0, 1)
    ]
    wdc = go(wd_own, wd.at[wd_rows, :], at(dc=1), "wd", 0)
    wx = {}
    for r in (1, 3, 2):
        wx[r] = go(w_loc.at[(x + r) % 4], w.at[w_rows, :], at(dx=r), "wx", r)
    wc = [go(w_loc.at[x], w.at[w_rows, :], at(dc=1), "wc", 0)]

    @pl.when(jnp.logical_not(inner))
    def _():
        zr_h[:, far] = jnp.zeros((4, 32, 512), BF)
        zr_p[:, far] = jnp.zeros((4, 32, 1024), BF)

    low, high = pl.ds(0, 512), pl.ds(512, 512)

    def spread_own(i):
        zh[i].wait_recv()
        src = acts.at[i, 0, 0]
        over_y = [go(src, acts.at[i, 0, m], at(dy=m), "y", i * 3 + m - 1) for m in (1, 3, 2)]
        over_x = [
            go(src.at[:, high], acts.at[i, k, 0, :, high], at(dx=k), "x1", i * 3 + k - 1)
            for k in (1, 3, 2)
        ]
        return over_y, over_x

    def spread_x(i, ks):
        for k in ks:
            src, dst = acts.at[i, 0, :, :, low], acts.at[i, k, :, :, low]
            slots[i, k] = go(src, dst, at(dx=k), "x", i * 3 + k - 1)

    def spread_y(i, copies):
        for cp in copies:
            cp.wait_recv()
        out = []
        for m in (1, 3, 2):
            src, dst = acts.at[i, pl.ds(1, 3), 0, :, high], acts.at[i, pl.ds(1, 3), m, :, high]
            out.append(go(src, dst, at(dy=m), "y2", i * 3 + m - 1))
        rights[i] = out

    def slot_ready(i, k):
        for cp in rights[i]:
            cp.wait_recv()
        rights[i] = []
        slots[i, k].wait_recv()

    slots, rights = {}, {}

    def scatter(k, src, dst, relay, name, relay_name):
        for m in range(4):
            rows = src.at[k, pl.ds(32 * m, 32)]
            direct = (z == 1) if m == 0 else (z == 2) if m == 3 else (z != m)
            go_if(direct, rows, dst.at[k, z], (gx, gy, m), name, k * 4 + m, k * 4 + z)
            if m in (0, 3):
                go_if(z == 3 - m, rows, relay.at[k], (gx, gy, via), relay_name, k)

    def hidden_grad(k):
        def tile(j, carry):
            rows = pl.ds(pl.multiple_of(j * 256, 256), 256)
            part = dot_nt(acts[0, k].reshape(128, 1024), wd[rows, :])
            zs_h[k, :, rows] = part.astype(BF)
            parts[k, :, pl.ds(pl.multiple_of(j * 256 + 1024, 256), 256)] = part
            return carry

        lax.fori_loop(0, 2, tile, 0, unroll=True)
        scatter(k, zs_h, zr_h, rl_h, "rh", "lh")

    def gate_up(k):
        def tile(j, carry):
            cols = pl.ds(pl.multiple_of(j * 256, 256), 256)
            part = dot_nn(acts[1, k].reshape(128, 1024), w[:, cols])
            zs_p[k, :, cols] = part.astype(BF)
            parts[k, :, cols] = part
            return carry

        lax.fori_loop(0, 4, tile, 0, unroll=True)
        scatter(k, zs_p, zr_p, rl_p, "rp", "lp")

    def relay(k):
        rows = pl.ds(pl.multiple_of(relay_to * 32, 32), 32)

        @pl.when(inner)
        def _():
            copy(rl_h.at[k], rl_h.at[k], (gx, gy, 3 - relay_to), "lh", k).wait_recv()
            zs_h[k, rows, :] = (parts[k, rows, 1024:1536] + rl_h[k].astype(F32)).astype(BF)
            copy(rl_p.at[k], rl_p.at[k], (gx, gy, 3 - relay_to), "lp", k).wait_recv()
            zs_p[k, rows, :] = (parts[k, rows, 0:1024] + rl_p[k].astype(F32)).astype(BF)

        for m in (0, 3):
            sel = z == (2 if m == 0 else 1)
            piece = pl.ds(32 * m, 32)
            go_if(sel, zs_h.at[k, piece], zr_h.at[k, z], (gx, gy, m), "rh", k * 4 + m, k * 4 + z)
            go_if(sel, zs_p.at[k, piece], zr_p.at[k, z], (gx, gy, m), "rp", k * 4 + m, k * 4 + z)

    def mix(k):
        for s in range(4):
            cond = (z != s) & (z != 3 - s) if s in (0, 3) else z != s
            wait_if(cond, zs_h.at[k, pl.ds(0, 32)], zr_h.at[k, s], (gx, gy, s), "rh", k * 4 + s)
            wait_if(cond, zs_p.at[k, pl.ds(0, 32)], zr_p.at[k, s], (gx, gy, s), "rp", k * 4 + s)
        mine = pl.ds(pl.multiple_of(z * 32, 32), 32)
        out = pl.ds(pl.multiple_of(z * 32 + 128 * k, 32), 32)

        def tile(j, carry):
            def total(got, off, skip):
                here = pl.ds(pl.multiple_of(j * 128 + off, 128), 128)
                mid = pl.ds(pl.multiple_of(j * 128 + off + skip, 128), 128)
                return (
                    (parts[k, mine, mid] + got[k, (z + 1) % 4, :, here].astype(F32))
                    + (got[k, (z + 2) % 4, :, here].astype(F32) + got[k, (z + 3) % 4, :, here].astype(F32))
                )

            up = total(zr_p, 0, 0)
            gate = total(zr_p, 512, 0)
            grad = total(zr_h, 0, 1024)
            sigma = jax.nn.sigmoid(gate)
            swish = gate * sigma

            def put(n, value):
                mids[out, pl.ds(pl.multiple_of(j * 128 + 512 * n, 128), 128)] = value.astype(BF)

            put(0, grad * swish)
            put(1, grad * up * sigma * (1.0 + gate * (1.0 - sigma)))
            put(2, swish * up)
            return carry

        lax.fori_loop(0, 4, tile, 0, unroll=True)
        block = mids.at[out, :]
        for m in range(4):
            cond = (z != m) & (z != 3 - m) if m in (0, 3) else z != m
            go_if(cond, block, block, (gx, gy, m), "ag", k * 4 + m, k * 4 + z)

    def forward(k):
        for m in (0, 3):
            sel = z == (1 if m == 0 else 2)
            block = mids.at[pl.ds(128 * k + 32 * (3 - m), 32), :]
            wait_if(sel, block, block, (gx, gy, 3 - m), "ag", k * 4 + 3 - m)
            go_if(sel, block, block, (gx, gy, m), "af", k, k * 4 - LAYOUT["af"] + LAYOUT["ag"] + 3 - m)

    def arrived(k):
        for s in range(4):
            cond = z != s
            if s == 0:
                cond = cond & (z != 2)
            if s == 3:
                cond = cond & (z != 1)
            block = mids.at[pl.ds(128 * k + 32 * s, 32), :]
            wait_if(cond, block, block, (gx, gy, s), "ag", k * 4 + s)

    def out_block(n, k):
        slot = pl.ds(128 * k, 128)

        def tile(j):
            cols = slice(256 * j, 256 * (j + 1))
            if n == 0:
                part = dot_nt(mids[slot, 0:1024], w[cols, :])
            else:
                part = dot_nn(mids[slot, 1024:1536], wd[:, cols])
            if k or j >= 2:
                o_send[n, k, :, cols] = part.astype(BF)
            if k == 0:
                o_own[n, :, cols] = part
            elif j >= 2:
                p_own[n, k, :, 256 * (j - 2):256 * (j - 1)] = part[0:32]

        for j in range(4):
            tile(j)
        if k:
            go(o_send.at[n, k, :, low], o_recv.at[n, k], at(dx=4 - k), "ox", n * 4 + k)
        for m in (1, 3, 2):
            src = o_send.at[n, k, pl.ds(32 * m, 32), high]
            go(src, p_recv.at[n, k, m], at(dy=4 - m), "py", n * 16 + k * 4 + m)

    def slot_cols(k):
        return slice(128 * k, 128 * (k + 1))

    def project(k):
        arrived(k)
        out_block(0, k)
        out_block(1, k)
        for j in range(12):
            mids_t[128 * j:128 * (j + 1), slot_cols(k)] = mids[slot_cols(k), 128 * j:128 * (j + 1)].T

    cot_y, cot_x = spread_own(0)
    tok_y, tok_x = spread_own(1)
    for cp in cot_y:
        cp.wait_recv()
    spread_x(0, (1, 3))
    wdc.wait_recv()
    hidden_grad(0)
    for cp in tok_y:
        cp.wait_recv()
    spread_x(1, (1, 3))
    spread_y(0, cot_x)
    spread_y(1, tok_x)
    for r in (1, 3, 2):
        wx[r].wait_recv()
        rows = pl.ds(pl.multiple_of(((x - r + 4) % 4 * 2 + c) * 128, 128), 128)
        wc.append(go(w.at[rows, :], w.at[rows, :], at(dc=1), "wc", r))
    spread_x(0, (2,))
    spread_x(1, (2,))
    for cp in wc:
        cp.wait_recv()
    gate_up(0)

    def slot_h(k):
        slot_ready(0, k)
        hidden_grad(k)

    def slot_p(k):
        slot_ready(1, k)
        gate_up(k)

    steps = {"H": slot_h, "P": slot_p, "R": relay, "D": mix, "F": forward, "G": project}
    for step in ORDER.split():
        steps[step[0]](int(step[1]))

    early = list(started), list(pending)
    del started[:], pending[:]

    def drain(copies, conds):
        for cp in copies:
            cp.wait_send()
        for cond, args in conds:
            @pl.when(cond)
            def _():
                copy(*args).wait_send()

    def token_cols(to, side):
        cols = pl.ds(pl.multiple_of((to * 2 + side) * 128, 128), 128)
        return acts[1, :, :, :, cols].reshape(512, 128)

    gc = {}
    for r in (1, 3, 2, 0):
        to = (x + r) % 4
        both = jnp.concatenate([token_cols(to, oc), token_cols(to, c)], axis=1)
        for n in range(4):
            part = dot_nn(mids_t[256 * n:256 * (n + 1)], both) * factor
            gc_send[r, 256 * n:256 * (n + 1), :] = part[:, 0:128].astype(BF)
            g_acc[r, 256 * n:256 * (n + 1), :] = part[:, 128:256]
        gc[r] = go(gc_send.at[r], gc_recv.at[r], at(dc=1), "gc", r)
    for r in (1, 3, 2):
        gc[r].wait_recv()
        gx_send[r] = (g_acc[r] + gc_recv[r].astype(F32)).astype(BF)
        go(gx_send.at[r], gx_recv.at[x], at(dx=r), "gx", r)

    drain(*early)
    theirs = pl.ds(pl.multiple_of(oc * 256 + 1024, 256), 256)
    ours = pl.ds(pl.multiple_of(c * 256 + 1024, 256), 256)

    def down_theirs(j, carry):
        cols = pl.ds(pl.multiple_of(j * 256, 256), 256)
        gd_send[:, cols] = (dot_nn(mids_t[theirs, :], acts[0, :, :, :, cols].reshape(512, 256)) * factor).astype(BF)
        return carry

    lax.fori_loop(0, 4, down_theirs, 0, unroll=True)
    gd = go(gd_send, gd_recv, at(dc=1), "gd", 0)

    oy, px = {}, {}
    for n in (0, 1):
        for k in range(4):
            for m in (1, 2, 3):
                src = o_send.at[n, k, pl.ds(32 * m, 32), high]
                copy(src, p_recv.at[n, k, m], at(dy=4 - m), "py", n * 16 + k * 4 + m).wait_recv()
            mine = p_own[n, k] if k else o_own[n, 0:32, 512:1024]
            p_sum[n, k] = (mine + p_recv[n, k, 1].astype(F32)) + (
                p_recv[n, k, 2].astype(F32) + p_recv[n, k, 3].astype(F32)
            )
            if k:
                px[n, k] = go(p_sum.at[n, k], px_recv.at[n, k], at(dx=4 - k), "px", n * 4 + k)
        for k in (1, 2, 3):
            src = o_send.at[n, k, :, low]
            copy(src, o_recv.at[n, k], at(dx=4 - k), "ox", n * 4 + k).wait_recv()
        y_own[n] = (o_own[n, :, 0:512] + o_recv[n, 1].astype(F32)) + (
            o_recv[n, 2].astype(F32) + o_recv[n, 3].astype(F32)
        )
        for m in (1, 3, 2):
            oy[n, m] = go(
                y_own.at[n, pl.ds(32 * m, 32), :], y_recv.at[n, m], at(dy=4 - m), "oy", n * 4 + m
            )

    def down_ours(j, carry):
        cols = pl.ds(pl.multiple_of(j * 256, 256), 256)
        gd_own[:, cols] = dot_nn(mids_t[ours, :], acts[0, :, :, :, cols].reshape(512, 256)) * factor
        return carry

    lax.fori_loop(0, 4, down_ours, 0, unroll=True)
    gd.wait_recv()
    gdown_ref[...] = gd_own[0:UNIT, :] + gd_recv[0:UNIT, :].astype(F32)

    oz = []
    for n in (0, 1):
        for m in (1, 2, 3):
            oy[n, m].wait_recv()
        z_send[n, :, 0:512] = (y_own[n, 0:32, :] + y_recv[n, 1]) + (y_recv[n, 2] + y_recv[n, 3])
        for k in (1, 2, 3):
            px[n, k].wait_recv()
        z_send[n, :, 512:1024] = (p_sum[n, 0] + px_recv[n, 1]) + (px_recv[n, 2] + px_recv[n, 3])
        oz.append(go(z_send.at[n, pl.ds(16, 16), :], z_recv.at[n], at(dh=1), "oz", n))

    gc[0].wait_recv()
    for r in (1, 2, 3):
        slot = (x - r + 4) % 4
        copy(gx_send.at[r], gx_recv.at[slot], at(dx=r), "gx", r).wait_recv()
    for p in range(4):
        @pl.when(x == p)
        def _():
            g_out[...] = g_acc[0] + gc_recv[0].astype(F32)

        @pl.when(x != p)
        def _():
            g_out[...] = gx_recv[p].astype(F32)

        for n, out in ((0, gup_ref), (1, ggate_ref)):
            for j in (0, 1):
                row = UNIT * (2 * p + j)
                out[row:row + UNIT, :] = g_out[512 * n + 256 * j:512 * n + 256 * j + UNIT, :]

    for n, out in ((0, gtok_ref), (1, mixed_ref)):
        oz[n].wait_recv()
        out[...] = (z_send[n, 0:16, :] + z_recv[n]).astype(BF)

    drain(started, pending)


def write_out(*refs):
    sems = refs[10]
    copies = [pltpu.make_async_copy(refs[i], refs[5 + i], sems.at[i]) for i in range(5)]
    for cp in copies:
        cp.start()
    for cp in copies:
        cp.wait()


def body(tokens, gate_weight, up_weight, down_weight, cotangent):
    vmem = pl.BlockSpec(memory_space=pltpu.VMEM)
    factor = 1.0 / math.sqrt(1024)
    anywhere = pl.BlockSpec(memory_space=pl.ANY)
    results = pl.pallas_call(
        functools.partial(kernel, factor),
        name="swiglu",
        out_shape=(
            jax.ShapeDtypeStruct((16, 1024), BF),
            jax.ShapeDtypeStruct((16, 1024), BF),
            jax.ShapeDtypeStruct((1848, 128), F32),
            jax.ShapeDtypeStruct((1848, 128), F32),
            jax.ShapeDtypeStruct((UNIT, 1024), F32),
        ),
        in_specs=[anywhere, anywhere, vmem, vmem, anywhere],
        out_specs=[vmem] * 5,
        scratch_shapes=[
            pltpu.VMEM((2, 4, 4, 32, 1024), BF),
            pltpu.VMEM((4, 128, 1024), BF),
            pltpu.VMEM((1024, 1024), BF),
            pltpu.VMEM((512, 1024), BF),
            pltpu.VMEM((4, 128, 1536), F32),
            pltpu.VMEM((4, 128, 512), BF),
            pltpu.VMEM((4, 4, 32, 512), BF),
            pltpu.VMEM((4, 32, 512), BF),
            pltpu.VMEM((4, 128, 1024), BF),
            pltpu.VMEM((4, 4, 32, 1024), BF),
            pltpu.VMEM((4, 32, 1024), BF),
            pltpu.VMEM((512, 1536), BF),
            pltpu.VMEM((1536, 512), BF),
            pltpu.VMEM((16, 1024), BF),
            pltpu.VMEM((16, 1024), BF),
            pltpu.VMEM((UNIT, 1024), BF),
            pltpu.VMEM((256, 1024), BF),
            pltpu.VMEM((2, 4, 128, 1024), BF),
            pltpu.VMEM((2, 4, 128, 512), BF),
            pltpu.VMEM((2, 128, 1024), F32),
            pltpu.VMEM((2, 4, 32, 512), F32),
            pltpu.VMEM((2, 4, 4, 32, 512), BF),
            pltpu.VMEM((2, 4, 32, 512), F32),
            pltpu.VMEM((2, 4, 32, 512), F32),
            pltpu.VMEM((2, 128, 512), F32),
            pltpu.VMEM((2, 4, 32, 512), F32),
            pltpu.VMEM((2, 32, 1024), F32),
            pltpu.VMEM((2, 16, 1024), F32),
            pltpu.VMEM((4, 1024, 128), BF),
            pltpu.VMEM((4, 1024, 128), BF),
            pltpu.VMEM((4, 1024, 128), F32),
            pltpu.VMEM((1024, 128), F32),
            pltpu.VMEM((4, 1024, 128), BF),
            pltpu.VMEM((4, 1024, 128), BF),
            pltpu.VMEM((256, 1024), BF),
            pltpu.VMEM((256, 1024), BF),
            pltpu.VMEM((256, 1024), F32),
            pltpu.SemaphoreType.DMA((COUNT,)),
            pltpu.SemaphoreType.DMA((COUNT,)),
            pltpu.SemaphoreType.DMA((3,)),
        ],
        compiler_params=pltpu.CompilerParams(
            collective_id=1, has_side_effects=True, vmem_limit_bytes=48 << 20
        ),
    )(tokens, cotangent, gate_weight, up_weight, down_weight)
    mixed, gtok, ggate, gup, gdown = pl.pallas_call(
        write_out,
        name="write_out",
        out_shape=tuple(jax.ShapeDtypeStruct(a.shape, a.dtype) for a in results),
        in_specs=[vmem] * 5,
        out_specs=[anywhere] * 5,
        scratch_shapes=[pltpu.SemaphoreType.DMA((5,))],
        compiler_params=pltpu.CompilerParams(vmem_limit_bytes=16 << 20),
    )(*results)
    return mixed, gtok, ggate.T, gup.T, gdown


def solution(mesh):
    in_specs = (
        P(("gy", "gx"), "gz"),
        P(("gz", "gy"), "gx"),
        P(("gz", "gy"), "gx"),
        P(("gx", "gy"), "gz"),
        P(("gy", "gx"), "gz"),
    )
    out_specs = (
        P(("gy", "gx"), "gz"),
        P(("gy", "gx"), "gz"),
        P(("gz", "gy"), "gx"),
        P(("gz", "gy"), "gx"),
        P(("gx", "gy"), "gz"),
    )
    return jax.shard_map(body, mesh=mesh, in_specs=in_specs, out_specs=out_specs, check_vma=False)
```

time: 130 us -> 120 us (0.923)
  local copies, waits for them, and re-layouts: 8.8 us -> 2.33 us
  Pallas kernels: 119 us -> 116 us
    unnamed x18 -> x10, local copies, waits for them, and re-layouts: 7.76 us -> 2.33 us
    pallas_call x1, Pallas kernels: 119 us -> 115 us  [body(): pl.pallas_call(functools.partial(kernel, factor), name='swiglu', out_shap...]
    pallas_call x0 -> x1, Pallas kernels: none -> 1.62 us  [body(): pl.pallas_call(write_out, name='write_out', out_shape=tuple((jax.ShapeDty...]
where the time goes in v3:
time: 120 us; the launch traced here: 119 us
  Pallas kernels  116 us (97%)
  local copies, waits for them, and re-layouts  2.33 us (2%)
    pallas_call x1, Pallas kernels, body(): pl.pallas_call(functools.partial(kernel, factor), name='swiglu', out_shap...  115 us

profile of v3, /device:TPU:40, one launch (start us, length us, event | category | flops | bytes accessed | tf_op | source)
XLA Modules:
  0.0 119.4 jit_solution(568456497336055693)
XLA Ops:
  0.6 0.0 copy-start.3
  0.6 1.3 %copy.10.gw_ref = bf16[128,1848]{1,0:T(8,128)(2,1)S(1)} copy(bf16[128,1848]{0,1:T(8,128)(2,1)} %param.6) | data formatting | bytes 946176 | tf_op args[1]
  2.0 0.0 copy-done.3
  2.0 0.0 copy-start
  2.0 0.0 copy-start.1
  2.0 0.0 copy-start.2
  2.0 0.3 copy.11.uw_ref
  2.3 0.7 copy-done
  3.0 0.0 copy-done.1
  3.0 0.0 copy-done.2
  3.0 114.7 %swiglu.1 = (bf16[16,1024]{1,0:T(8,128)(2,1)S(1)}, bf16[16,1024]{1,0:T(8,128)(2,1)S(1)}, f32[1848,128]{1,0:T(8,128)S(1)}, f32[1848,128]{1,0:T(8,128)S(1)}, f32[231,1024]{1,0:T(8,128)S(1)}) custom-call(bf16[16,1024]{1,0:T(8,128)(2,1)S(1)} %copy-done.1, bf16[16,1024]{1,0:T(8,128)(2,1)S(1)} %copy-done.2, bf16[128,1848]{1,0:T(8,128)(2,1)S(1)} %copy.10.gw_ref, ...), custom_call_target="tpu_custom_call" | custom-call | tf_op jit(solution)/shard_map/swiglu/pallas_call | solution.py:459
  117.8 1.6 %write_out.1 = (bf16[16,1024]{1,0:T(8,128)(2,1)}, bf16[16,1024]{1,0:T(8,128)(2,1)}, f32[1848,128]{1,0:T(8,128)}, f32[1848,128]{1,0:T(8,128)}, f32[231,1024]{1,0:T(8,128)}) custom-call(bf16[16,1024]{1,0:T(8,128)(2,1)S(1)} %get-tuple-element.15.refs_0_, bf16[16,1024]{1,0:T(8,128)(2,1)S(1)} %get-tuple-element.16.refs_1_, ...), custom_call_target="tpu_custom_call" | custom-call | tf_op jit(solution)/shard_map/write_out/pallas_call | solution.py:517
Async XLA Ops:
  0.6 1.3 %copy-start.3 = (bf16[128,1848]{0,1:T(8,128)(2,1)S(1)}, bf16[128,1848]{0,1:T(8,128)(2,1)}, u32[]{:S(2)}) copy-start(bf16[128,1848]{0,1:T(8,128)(2,1)} %param.7) | copy-start | bytes 1419268
  2.0 1.0 copy-start
  2.0 1.0 copy-start.1
  2.0 1.0 copy-start.2

commit v4 on v3

--- a/solution.py
+++ b/solution.py
@@ -12,6 +12,8 @@
 F32 = jnp.float32
 ORDER = "H1 P1 R0 H3 P3 D0 H2 P2 R1 R3 F0 D1 R2 D3 F1 G0 D2 F3 G1 F2 G3 G2"
 MESH_ID = pl.DeviceIdType.MESH
+LOW = 512
+HIGH = 1024 - LOW
 UNIT = 231
 
 
@@ -38,7 +40,7 @@
     factor,
     tok_ref, cot_ref, gw_ref, uw_ref, wd_ref,
     mixed_ref, gtok_ref, ggate_ref, gup_ref, gdown_ref,
-    acts, w_loc, w, wd, parts, zs_h, zr_h, rl_h, zs_p, zr_p, rl_p, mids, mids_t, tok_in, cot_in, wd_in, wd_own,
+    acts, w_loc, w, wd, parts, zs_h, zr_h, rl_h, zs_p, zr_p, rl_p, mids, mids_t, gw_in, uw_in, tok_in, cot_in, wd_in, wd_own,
     o_send, o_recv, o_own, p_own, p_recv, p_sum, px_recv, y_own, y_recv, z_send, z_recv,
     gc_send, gc_recv, g_acc, g_out, gx_send, gx_recv, gd_send, gd_recv, gd_own,
     send, recv, local,
@@ -93,7 +95,7 @@
     )
     loads = [
         pltpu.make_async_copy(src, dst, local.at[i])
-        for i, (src, dst) in enumerate(((cot_ref, cot_in), (tok_ref, tok_in), (wd_ref, wd_in)))
+        for i, (src, dst) in enumerate(((uw_ref, uw_in), (gw_ref, gw_in), (cot_ref, cot_in), (tok_ref, tok_in), (wd_ref, wd_in)))
     ]
     for load in loads:
         load.start()
@@ -101,15 +103,17 @@
     for who in peers:
         pl.semaphore_signal(barrier, inc=1, device_id=who, device_id_type=MESH_ID)
     zeros = jnp.zeros((128, 256), BF)
-    for n, ref in ((0, uw_ref), (1, gw_ref)):
+    for n, ref in ((0, uw_in), (1, gw_in)):
+        loads[n].wait()
+        flat = ref[...].T
         for j in range(8):
             base = n * 512 + (j % 2) * 256
             w_loc[j // 2, :, base:base + 256] = zeros
-            w_loc[j // 2, :, base:base + UNIT] = ref[:, UNIT * j:UNIT * (j + 1)]
+            w_loc[j // 2, :, base:base + UNIT] = flat[:, UNIT * j:UNIT * (j + 1)]
     row_own = pl.multiple_of((x * 2 + c) * 128, 128)
     w_rows = pl.ds(row_own, 128)
     w[w_rows, :] = w_loc[x]
-    for load in loads:
+    for load in loads[2:]:
         load.wait()
     acts[0, 0, 0, 0:16, :] = cot_in[...]
     acts[1, 0, 0, 0:16, :] = tok_in[...]
@@ -133,7 +137,7 @@
         zr_h[:, far] = jnp.zeros((4, 32, 512), BF)
         zr_p[:, far] = jnp.zeros((4, 32, 1024), BF)
 
-    low, high = pl.ds(0, 512), pl.ds(512, 512)
+    low, high = pl.ds(0, LOW), pl.ds(LOW, HIGH)
 
     def spread_own(i):
         zh[i].wait_recv()
@@ -276,12 +280,12 @@
                 part = dot_nt(mids[slot, 0:1024], w[cols, :])
             else:
                 part = dot_nn(mids[slot, 1024:1536], wd[:, cols])
-            if k or j >= 2:
+            if k or 256 * j >= LOW:
                 o_send[n, k, :, cols] = part.astype(BF)
             if k == 0:
                 o_own[n, :, cols] = part
-            elif j >= 2:
-                p_own[n, k, :, 256 * (j - 2):256 * (j - 1)] = part[0:32]
+            elif 256 * j >= LOW:
+                p_own[n, k, :, 256 * j - LOW:256 * (j + 1) - LOW] = part[0:32]
 
         for j in range(4):
             tile(j)
@@ -356,8 +360,8 @@
         both = jnp.concatenate([token_cols(to, oc), token_cols(to, c)], axis=1)
         for n in range(4):
             part = dot_nn(mids_t[256 * n:256 * (n + 1)], both) * factor
-            gc_send[r, 256 * n:256 * (n + 1), :] = part[:, 0:128].astype(BF)
-            g_acc[r, 256 * n:256 * (n + 1), :] = part[:, 128:256]
+            gc_send[r, n] = part[0:240, 0:128].astype(BF)
+            g_acc[r, n] = part[0:240, 128:256]
         gc[r] = go(gc_send.at[r], gc_recv.at[r], at(dc=1), "gc", r)
     for r in (1, 3, 2):
         gc[r].wait_recv()
@@ -382,7 +386,7 @@
             for m in (1, 2, 3):
                 src = o_send.at[n, k, pl.ds(32 * m, 32), high]
                 copy(src, p_recv.at[n, k, m], at(dy=4 - m), "py", n * 16 + k * 4 + m).wait_recv()
-            mine = p_own[n, k] if k else o_own[n, 0:32, 512:1024]
+            mine = p_own[n, k] if k else o_own[n, 0:32, LOW:1024]
             p_sum[n, k] = (mine + p_recv[n, k, 1].astype(F32)) + (
                 p_recv[n, k, 2].astype(F32) + p_recv[n, k, 3].astype(F32)
             )
@@ -391,7 +395,7 @@
         for k in (1, 2, 3):
             src = o_send.at[n, k, :, low]
             copy(src, o_recv.at[n, k], at(dx=4 - k), "ox", n * 4 + k).wait_recv()
-        y_own[n] = (o_own[n, :, 0:512] + o_recv[n, 1].astype(F32)) + (
+        y_own[n] = (o_own[n, :, 0:LOW] + o_recv[n, 1].astype(F32)) + (
             o_recv[n, 2].astype(F32) + o_recv[n, 3].astype(F32)
         )
         for m in (1, 3, 2):
@@ -412,10 +416,10 @@
     for n in (0, 1):
         for m in (1, 2, 3):
             oy[n, m].wait_recv()
-        z_send[n, :, 0:512] = (y_own[n, 0:32, :] + y_recv[n, 1]) + (y_recv[n, 2] + y_recv[n, 3])
+        z_send[n, :, 0:LOW] = (y_own[n, 0:32, :] + y_recv[n, 1]) + (y_recv[n, 2] + y_recv[n, 3])
         for k in (1, 2, 3):
             px[n, k].wait_recv()
-        z_send[n, :, 512:1024] = (p_sum[n, 0] + px_recv[n, 1]) + (px_recv[n, 2] + px_recv[n, 3])
+        z_send[n, :, LOW:1024] = (p_sum[n, 0] + px_recv[n, 1]) + (px_recv[n, 2] + px_recv[n, 3])
         oz.append(go(z_send.at[n, pl.ds(16, 16), :], z_recv.at[n], at(dh=1), "oz", n))
 
     gc[0].wait_recv()
@@ -434,7 +438,7 @@
         for n, out in ((0, gup_ref), (1, ggate_ref)):
             for j in (0, 1):
                 row = UNIT * (2 * p + j)
-                out[row:row + UNIT, :] = g_out[512 * n + 256 * j:512 * n + 256 * j + UNIT, :]
+                out[row:row + UNIT, :] = g_out[2 * n + j, 0:UNIT, :]
 
     for n, out in ((0, gtok_ref), (1, mixed_ref)):
         oz[n].wait_recv()
@@ -466,7 +470,7 @@
             jax.ShapeDtypeStruct((1848, 128), F32),
             jax.ShapeDtypeStruct((UNIT, 1024), F32),
         ),
-        in_specs=[anywhere, anywhere, vmem, vmem, anywhere],
+        in_specs=[anywhere] * 5,
         out_specs=[vmem] * 5,
         scratch_shapes=[
             pltpu.VMEM((2, 4, 4, 32, 1024), BF),
@@ -482,38 +486,40 @@
             pltpu.VMEM((4, 32, 1024), BF),
             pltpu.VMEM((512, 1536), BF),
             pltpu.VMEM((1536, 512), BF),
+            pltpu.VMEM((1848, 128), BF),
+            pltpu.VMEM((1848, 128), BF),
             pltpu.VMEM((16, 1024), BF),
             pltpu.VMEM((16, 1024), BF),
             pltpu.VMEM((UNIT, 1024), BF),
             pltpu.VMEM((256, 1024), BF),
             pltpu.VMEM((2, 4, 128, 1024), BF),
-            pltpu.VMEM((2, 4, 128, 512), BF),
+            pltpu.VMEM((2, 4, 128, LOW), BF),
             pltpu.VMEM((2, 128, 1024), F32),
-            pltpu.VMEM((2, 4, 32, 512), F32),
-            pltpu.VMEM((2, 4, 4, 32, 512), BF),
-            pltpu.VMEM((2, 4, 32, 512), F32),
-            pltpu.VMEM((2, 4, 32, 512), F32),
-            pltpu.VMEM((2, 128, 512), F32),
-            pltpu.VMEM((2, 4, 32, 512), F32),
+            pltpu.VMEM((2, 4, 32, HIGH), F32),
+            pltpu.VMEM((2, 4, 4, 32, HIGH), BF),
+            pltpu.VMEM((2, 4, 32, HIGH), F32),
+            pltpu.VMEM((2, 4, 32, HIGH), F32),
+            pltpu.VMEM((2, 128, LOW), F32),
+            pltpu.VMEM((2, 4, 32, LOW), F32),
             pltpu.VMEM((2, 32, 1024), F32),
             pltpu.VMEM((2, 16, 1024), F32),
-            pltpu.VMEM((4, 1024, 128), BF),
-            pltpu.VMEM((4, 1024, 128), BF),
-            pltpu.VMEM((4, 1024, 128), F32),
-            pltpu.VMEM((1024, 128), F32),
-            pltpu.VMEM((4, 1024, 128), BF),
-            pltpu.VMEM((4, 1024, 128), BF),
+            pltpu.VMEM((4, 4, 240, 128), BF),
+            pltpu.VMEM((4, 4, 240, 128), BF),
+            pltpu.VMEM((4, 4, 240, 128), F32),
+            pltpu.VMEM((4, 240, 128), F32),
+            pltpu.VMEM((4, 4, 240, 128), BF),
+            pltpu.VMEM((4, 4, 240, 128), BF),
             pltpu.VMEM((256, 1024), BF),
             pltpu.VMEM((256, 1024), BF),
             pltpu.VMEM((256, 1024), F32),
             pltpu.SemaphoreType.DMA((COUNT,)),
             pltpu.SemaphoreType.DMA((COUNT,)),
-            pltpu.SemaphoreType.DMA((3,)),
+            pltpu.SemaphoreType.DMA((5,)),
         ],
         compiler_params=pltpu.CompilerParams(
             collective_id=1, has_side_effects=True, vmem_limit_bytes=48 << 20
         ),
-    )(tokens, cotangent, gate_weight, up_weight, down_weight)
+    )(tokens, cotangent, gate_weight.T, up_weight.T, down_weight)
     mixed, gtok, ggate, gup, gdown = pl.pallas_call(
         write_out,
         name="write_out",

time: 120 us -> 122 us (1.017)
  local copies, waits for them, and re-layouts: 2.33 us -> 4.58 us
    unnamed x10, local copies, waits for them, and re-layouts: 2.33 us -> 4.58 us
where the time goes in v4:
time: 122 us; the launch traced here: 121 us
  Pallas kernels  116 us (95%)
  local copies, waits for them, and re-layouts  4.58 us (4%)
    pallas_call x1, Pallas kernels, body(): pl.pallas_call(functools.partial(kernel, factor), name='swiglu', out_shap...  115 us
    unnamed x10, local copies, waits for them, and re-layouts  4.58 us

profile of v4, /device:TPU:40, one launch (start us, length us, event | category | flops | bytes accessed | tf_op | source)
XLA Modules:
  0.0 121.5 jit_solution(4405407505087277450)
XLA Ops:
  0.6 0.0 copy-start
  0.6 1.0 copy-done
  1.7 0.0 copy-start.1
  1.7 1.0 copy-done.1
  2.7 0.0 copy-start.2
  2.7 1.0 copy-done.2
  3.7 0.0 copy-start.3
  3.7 0.8 copy-done.3
  4.5 0.0 copy-start.4
  4.5 0.8 copy-done.4
  5.2 114.6 %swiglu.1 = (bf16[16,1024]{1,0:T(8,128)(2,1)S(1)}, bf16[16,1024]{1,0:T(8,128)(2,1)S(1)}, f32[1848,128]{1,0:T(8,128)S(1)}, f32[1848,128]{1,0:T(8,128)S(1)}, f32[231,1024]{1,0:T(8,128)S(1)}) custom-call(bf16[16,1024]{1,0:T(8,128)(2,1)S(1)} %copy-done.3, bf16[16,1024]{1,0:T(8,128)(2,1)S(1)} %copy-done.4, bf16[1848,128]{1,0:T(8,128)(2,1)S(1)} %bitcast.4, ...), custom_call_target="tpu_custom_call" | custom-call | tf_op jit(solution)/shard_map/swiglu/pallas_call | solution.py:463
  119.8 1.6 %write_out.1 = (bf16[16,1024]{1,0:T(8,128)(2,1)}, bf16[16,1024]{1,0:T(8,128)(2,1)}, f32[1848,128]{1,0:T(8,128)}, f32[1848,128]{1,0:T(8,128)}, f32[231,1024]{1,0:T(8,128)}) custom-call(bf16[16,1024]{1,0:T(8,128)(2,1)S(1)} %get-tuple-element.15.refs_0_, bf16[16,1024]{1,0:T(8,128)(2,1)S(1)} %get-tuple-element.16.refs_1_, ...), custom_call_target="tpu_custom_call" | custom-call | tf_op jit(solution)/shard_map/write_out/pallas_call | solution.py:523
Async XLA Ops:
  0.6 1.0 copy-start
  1.7 1.0 copy-start.1
  2.7 1.0 copy-start.2
  3.7 0.8 copy-start.3
  4.5 0.8 copy-start.4

commit v5 on v4

--- a/solution.py
+++ b/solution.py
@@ -40,7 +40,7 @@
     factor,
     tok_ref, cot_ref, gw_ref, uw_ref, wd_ref,
     mixed_ref, gtok_ref, ggate_ref, gup_ref, gdown_ref,
-    acts, w_loc, w, wd, parts, zs_h, zr_h, rl_h, zs_p, zr_p, rl_p, mids, mids_t, gw_in, uw_in, tok_in, cot_in, wd_in, wd_own,
+    acts, w_loc, w, wd, parts, zs_h, zr_h, rl_h, zs_p, zr_p, rl_p, mids, mids_t, tok_in, cot_in, wd_in, wd_own,
     o_send, o_recv, o_own, p_own, p_recv, p_sum, px_recv, y_own, y_recv, z_send, z_recv,
     gc_send, gc_recv, g_acc, g_out, gx_send, gx_recv, gd_send, gd_recv, gd_own,
     send, recv, local,
@@ -95,7 +95,7 @@
     )
     loads = [
         pltpu.make_async_copy(src, dst, local.at[i])
-        for i, (src, dst) in enumerate(((uw_ref, uw_in), (gw_ref, gw_in), (cot_ref, cot_in), (tok_ref, tok_in), (wd_ref, wd_in)))
+        for i, (src, dst) in enumerate(((cot_ref, cot_in), (tok_ref, tok_in), (wd_ref, wd_in)))
     ]
     for load in loads:
         load.start()
@@ -103,17 +103,15 @@
     for who in peers:
         pl.semaphore_signal(barrier, inc=1, device_id=who, device_id_type=MESH_ID)
     zeros = jnp.zeros((128, 256), BF)
-    for n, ref in ((0, uw_in), (1, gw_in)):
-        loads[n].wait()
-        flat = ref[...].T
+    for n, ref in ((0, uw_ref), (1, gw_ref)):
         for j in range(8):
             base = n * 512 + (j % 2) * 256
             w_loc[j // 2, :, base:base + 256] = zeros
-            w_loc[j // 2, :, base:base + UNIT] = flat[:, UNIT * j:UNIT * (j + 1)]
+            w_loc[j // 2, :, base:base + UNIT] = ref[:, UNIT * j:UNIT * (j + 1)]
     row_own = pl.multiple_of((x * 2 + c) * 128, 128)
     w_rows = pl.ds(row_own, 128)
     w[w_rows, :] = w_loc[x]
-    for load in loads[2:]:
+    for load in loads:
         load.wait()
     acts[0, 0, 0, 0:16, :] = cot_in[...]
     acts[1, 0, 0, 0:16, :] = tok_in[...]
@@ -470,7 +468,7 @@
             jax.ShapeDtypeStruct((1848, 128), F32),
             jax.ShapeDtypeStruct((UNIT, 1024), F32),
         ),
-        in_specs=[anywhere] * 5,
+        in_specs=[anywhere, anywhere, vmem, vmem, anywhere],
         out_specs=[vmem] * 5,
         scratch_shapes=[
             pltpu.VMEM((2, 4, 4, 32, 1024), BF),
@@ -486,8 +484,6 @@
             pltpu.VMEM((4, 32, 1024), BF),
             pltpu.VMEM((512, 1536), BF),
             pltpu.VMEM((1536, 512), BF),
-            pltpu.VMEM((1848, 128), BF),
-            pltpu.VMEM((1848, 128), BF),
             pltpu.VMEM((16, 1024), BF),
             pltpu.VMEM((16, 1024), BF),
             pltpu.VMEM((UNIT, 1024), BF),
@@ -514,12 +510,12 @@
             pltpu.VMEM((256, 1024), F32),
             pltpu.SemaphoreType.DMA((COUNT,)),
             pltpu.SemaphoreType.DMA((COUNT,)),
-            pltpu.SemaphoreType.DMA((5,)),
+            pltpu.SemaphoreType.DMA((3,)),
         ],
         compiler_params=pltpu.CompilerParams(
             collective_id=1, has_side_effects=True, vmem_limit_bytes=48 << 20
         ),
-    )(tokens, cotangent, gate_weight.T, up_weight.T, down_weight)
+    )(tokens, cotangent, gate_weight, up_weight, down_weight)
     mixed, gtok, ggate, gup, gdown = pl.pallas_call(
         write_out,
         name="write_out",

time: 122 us -> 119 us (0.975)
  local copies, waits for them, and re-layouts: 4.58 us -> 2.33 us
    unnamed x10, local copies, waits for them, and re-layouts: 4.58 us -> 2.33 us
where the time goes in v5:
time: 119 us
  Pallas kernels  116 us (97%)
  local copies, waits for them, and re-layouts  2.33 us (2%)
    pallas_call x1, Pallas kernels, body(): pl.pallas_call(functools.partial(kernel, factor), name='swiglu', out_shap...  114 us

profile of v5, /device:TPU:40, one launch (start us, length us, event | category | flops | bytes accessed | tf_op | source)
XLA Modules:
  0.0 118.7 jit_solution(6887419376000468091)
XLA Ops:
  0.6 0.0 copy-start.3
  0.6 1.3 %copy.10.gw_ref = bf16[128,1848]{1,0:T(8,128)(2,1)S(1)} copy(bf16[128,1848]{0,1:T(8,128)(2,1)} %param.6) | data formatting | bytes 946176 | tf_op args[1]
  2.0 0.0 copy-done.3
  2.0 0.0 copy-start
  2.0 0.0 copy-start.1
  2.0 0.0 copy-start.2
  2.0 0.3 copy.11.uw_ref
  2.3 0.7 copy-done
  3.0 0.0 copy-done.1
  3.0 0.0 copy-done.2
  3.0 114.0 %swiglu.1 = (bf16[16,1024]{1,0:T(8,128)(2,1)S(1)}, bf16[16,1024]{1,0:T(8,128)(2,1)S(1)}, f32[1848,128]{1,0:T(8,128)S(1)}, f32[1848,128]{1,0:T(8,128)S(1)}, f32[231,1024]{1,0:T(8,128)S(1)}) custom-call(bf16[16,1024]{1,0:T(8,128)(2,1)S(1)} %copy-done.1, bf16[16,1024]{1,0:T(8,128)(2,1)S(1)} %copy-done.2, bf16[128,1848]{1,0:T(8,128)(2,1)S(1)} %copy.10.gw_ref, ...), custom_call_target="tpu_custom_call" | custom-call | tf_op jit(solution)/shard_map/swiglu/pallas_call | solution.py:461
  117.0 1.6 %write_out.1 = (bf16[16,1024]{1,0:T(8,128)(2,1)}, bf16[16,1024]{1,0:T(8,128)(2,1)}, f32[1848,128]{1,0:T(8,128)}, f32[1848,128]{1,0:T(8,128)}, f32[231,1024]{1,0:T(8,128)}) custom-call(bf16[16,1024]{1,0:T(8,128)(2,1)S(1)} %get-tuple-element.15.refs_0_, bf16[16,1024]{1,0:T(8,128)(2,1)S(1)} %get-tuple-element.16.refs_1_, ...), custom_call_target="tpu_custom_call" | custom-call | tf_op jit(solution)/shard_map/write_out/pallas_call | solution.py:519
Async XLA Ops:
  0.6 1.3 %copy-start.3 = (bf16[128,1848]{0,1:T(8,128)(2,1)S(1)}, bf16[128,1848]{0,1:T(8,128)(2,1)}, u32[]{:S(2)}) copy-start(bf16[128,1848]{0,1:T(8,128)(2,1)} %param.7) | copy-start | bytes 1419268
  2.0 1.0 copy-start
  2.0 1.0 copy-start.1
  2.0 1.0 copy-start.2
